TPU v7x, 32 devices: a whole 2x2x4 slice. The times are simulated.
32 devices in a mesh: groups: 2 (over y), graph: 8 (over z, x), mp: 2 (over core).
Axes of the slice: x: 2, y: 2, z: 4, core: 2. Of those that a mesh axis runs over, the one named last changes fastest.
Arguments:
- edges: bfloat16 [16384, 512], P(('groups', 'graph'), 'mp'), parts along dimension 0, may hold values from -6 to 6
- basis: bfloat16 [64, 32768], P(None, ('groups', 'graph')), parts along dimension 1, may hold values from -6 to 6
- w_basis: bfloat16 [64, 512], P(None, 'mp'), may hold values from -0.75 to 0.75
- w_up: bfloat16 [512, 512], P('mp'), may hold values from -0.25 to 0.25
- out_grad: bfloat16 [16384, 512], P(('groups', 'graph'), 'mp'), parts along dimension 0, may hold values from -6 to 6
- send_index: int32 [16, 256], P(('groups', 'graph')), parts along dimension 0, may hold values from 0 to 1023
- trip_slot: int32 [32768], P(('groups', 'graph')), parts along dimension 0, may hold values from 0 to 1279, as said below
- trip_out: int32 [32768], P(('groups', 'graph')), parts along dimension 0, may hold values from 0 to 1023
Outputs:
- grad_edges: bfloat16 [16384, 512], P(('groups', 'graph'), 'mp'), parts along dimension 0
- grad_w_up: float32 [1024, 512], P(('groups', 'mp')), parts along dimension 0
- grad_w_basis: float32 [128, 512], P('groups', 'mp'), parts along dimension 0
There are 2 independent parts, one for each index of `groups`. A program takes and returns all parts, laid end to end along the dimension named above; an argument that names none is the same for every part. Nothing has to cross between parts.
Inputs may be any that keep to these rules, and one draw needn't show every extreme that they name: `trip_slot`: A value v below 1024 is a local edge of the triplet's shard; a value v of 1024 or more names row (v - 1024) % 32 of the rows that graph shard (v - 1024) // 32 packs for this shard by send_index, and only live rows are named. Each shard has between 8 and 32 live rows for each peer; every shard has all 32 live for graph shard 0 and for the next shard.
All inputs are finite; a program needn't handle non-finite values.
Results may differ from a plain program's by a relative error of at most 0.0059.
Values may be sent and summed in bfloat16 or wider, within the bound.
No kernel may reach another device: no remote copies, remote signals or barrier semaphores. Data moves between devices by JAX's collectives and lax.ppermute only.
A program may use at most 64 MiB of HBM per device.

v0:
```python
import math

import jax
import jax.numpy as jnp
from jax import lax
from jax.sharding import PartitionSpec as P


def silu_slope(pre):
    sig = jax.nn.sigmoid(pre)
    return sig * (1.0 + pre * (1.0 - sig))


def one_hot(values, count, dtype):
    return (values[:, None] == jnp.arange(count, dtype=jnp.int32)[None, :]).astype(dtype)


def spread_sum(select, values):
    return lax.dot_general(
        select,
        values,
        (((0,), (0,)), ((), ())),
        precision=lax.Precision.HIGHEST,
        preferred_element_type=jnp.float32,
    )


def on_device(edges, basis, w_basis, w_up, out_grad, send_index, trip_slot, trip_out):
    n_graph = lax.axis_size("graph")
    local_rows, half_width = edges.shape
    capacity = send_index.shape[1] // n_graph
    edge_total = local_rows * n_graph
    trip_local = basis.shape[1]
    trip_total = trip_local * n_graph
    table_rows = local_rows + n_graph * capacity
    block_len = math.gcd(trip_local, 512)
    n_blocks = trip_local // block_len
    pack_select = one_hot(send_index[0], local_rows, jnp.bfloat16)
    packed = jnp.dot(pack_select, edges, preferred_element_type=jnp.float32).astype(jnp.bfloat16)
    received = lax.all_to_all(
        packed.reshape(n_graph, capacity, half_width),
        "graph",
        split_axis=0,
        concat_axis=0,
        tiled=True,
    )
    table = jnp.concatenate([edges, received.reshape(n_graph * capacity, half_width)], axis=0)
    agg_sum = jnp.zeros((local_rows, half_width), jnp.float32)
    kept_rows = []
    kept_proj = []
    for block in range(n_blocks):
        slots = trip_slot[block * block_len : (block + 1) * block_len]
        outs = trip_out[block * block_len : (block + 1) * block_len]
        bas = basis[:, block * block_len : (block + 1) * block_len]
        neighbour = jnp.dot(
            one_hot(slots, table_rows, jnp.bfloat16), table, preferred_element_type=jnp.float32
        )
        proj = lax.dot_general(
            bas, w_basis, (((0,), (0,)), ((), ())), preferred_element_type=jnp.float32
        )
        agg_sum = agg_sum + spread_sum(one_hot(outs, local_rows, jnp.float32), neighbour * proj)
        kept_rows.append(neighbour)
        kept_proj.append(proj)
    agg = agg_sum.astype(jnp.bfloat16)
    partial_value = jnp.dot(agg, w_up, preferred_element_type=jnp.float32)
    pre = lax.psum_scatter(partial_value, "mp", scatter_dimension=1, tiled=True)
    g_half = (out_grad.astype(jnp.float32) * silu_slope(pre)).astype(jnp.bfloat16)
    g_pre = lax.all_gather(g_half, "mp", axis=1, tiled=True)
    grad_up_local = lax.dot_general(
        agg, g_pre, (((0,), (0,)), ((), ())), preferred_element_type=jnp.float32
    ) * edge_total ** (-0.5)
    g_agg = lax.dot_general(
        g_pre, w_up, (((1,), (1,)), ((), ())), preferred_element_type=jnp.float32
    )
    grad_basis_sum = jnp.zeros((basis.shape[0], half_width), jnp.float32)
    slot_grad = jnp.zeros((table_rows, half_width), jnp.float32)
    for block in range(n_blocks):
        slots = trip_slot[block * block_len : (block + 1) * block_len]
        outs = trip_out[block * block_len : (block + 1) * block_len]
        bas = basis[:, block * block_len : (block + 1) * block_len]
        g_y = jnp.dot(
            one_hot(outs, local_rows, jnp.float32),
            g_agg,
            precision=lax.Precision.HIGHEST,
            preferred_element_type=jnp.float32,
        )
        tgrad = (g_y * kept_rows[block]).astype(jnp.bfloat16)
        grad_basis_sum = grad_basis_sum + jnp.dot(bas, tgrad, preferred_element_type=jnp.float32)
        slot_grad = slot_grad + spread_sum(
            one_hot(slots, table_rows, jnp.float32), g_y * kept_proj[block]
        )
    grad_basis_local = grad_basis_sum * trip_total ** (-0.5)
    grad_w_up, grad_w_basis = lax.psum((grad_up_local, grad_basis_local), "graph")
    outgoing = slot_grad[local_rows:].reshape(n_graph, capacity, half_width)
    returned = lax.all_to_all(outgoing, "graph", split_axis=0, concat_axis=0, tiled=True)
    back_rows = spread_sum(
        pack_select.astype(jnp.float32), returned.reshape(n_graph * capacity, half_width)
    )
    grad_edges = (slot_grad[:local_rows] + back_rows).astype(jnp.bfloat16)
    return (grad_edges, grad_w_up, grad_w_basis)


def solution(mesh):
    placed = (
        P(("groups", "graph"), "mp"),
        P(None, ("groups", "graph")),
        P(None, "mp"),
        P("mp", None),
        P(("groups", "graph"), "mp"),
        P(("groups", "graph"), None),
        P(("groups", "graph")),
        P(("groups", "graph")),
    )
    return jax.shard_map(
        on_device,
        mesh=mesh,
        in_specs=placed,
        out_specs=(P(("groups", "graph"), "mp"), P(("groups", "mp"), None), P("groups", "mp")),
        check_vma=False,
    )
```

profile of v0, /device:TPU:0, one launch (start us, length us, event | category | flops | bytes accessed | tf_op | source)
XLA Modules:
  0.0 170.4 jit_solution(2319663927314178580)
XLA Ops:
  7.2 2.1 %convolution_convert_fusion = bf16[256,256]{1,0:T(8,128)(2,1)} fusion(bf16[1024,256]{1,0:T(8,128)(2,1)} %param.8, s32[256]{0:T(256)} %bitcast.28), kind=kOutput, calls=%fused_computation.39 | convolution fusion | flops 134545408 | bytes 656384 | tf_op jit(solution)/shard_map/dot_general | solution.py:39
  9.4 7.3 %all-to-all-start = ((bf16[8,32,256]{2,1,0:T(8,128)(2,1)}), bf16[8,32,256]{2,1,0:T(8,128)(2,1)S(1)}, u32[]{:S(2)}, u32[]{:S(2)}) async-start(bf16[8,32,256]{2,1,0:T(8,128)(2,1)} %bitcast.1), calls=%async_computation | async-start | bytes 262144 | tf_op jit(solution)/shard_map/all_to_all | solution.py:40
  16.7 1.1 fusion.54
  17.8 1.1 fusion.57
  19.4 4.5 %all-to-all-done = bf16[8,32,256]{2,1,0:T(8,128)(2,1)S(1)} async-done(((bf16[8,32,256]{2,1,0:T(8,128)(2,1)}), bf16[8,32,256]{2,1,0:T(8,128)(2,1)S(1)}, u32[]{:S(2)}, u32[]{:S(2)}) %all-to-all-start) | async-done | bytes 131104 | tf_op jit(solution)/shard_map/all_to_all | solution.py:40
  26.5 1.9 %fusion.8 = f32[1024,256]{1,0:T(8,128)S(1)} fusion(s32[512]{0:T(512)S(1)} %get-tuple-element.8, f32[512,256]{1,0:T(8,128)S(1)} %fusion.1, f32[512,256]{1,0:T(8,128)S(1)} %fusion.51), kind=kOutput, calls=%fused_computation.17 | convolution fusion | flops 1611268096 | bytes 2099200 | tf_op jit(solution)/shard_map/dot_general | solution.py:19
  28.4 1.9 %fusion.6 = f32[1024,256]{1,0:T(8,128)S(1)} fusion(s32[512]{0:T(512)S(1)} %get-tuple-element.7, f32[512,256]{1,0:T(8,128)S(1)} %fusion, f32[512,256]{1,0:T(8,128)S(1)} %fusion.48), kind=kOutput, calls=%fused_computation.14 | convolution fusion | flops 1611268096 | bytes 2099200 | tf_op jit(solution)/shard_map/dot_general | solution.py:19
  30.3 1.9 %fusion.10 = f32[1024,256]{1,0:T(8,128)S(1)} fusion(s32[512]{0:T(512)S(1)} %get-tuple-element.6, f32[512,256]{1,0:T(8,128)S(1)} %fusion.2, f32[512,256]{1,0:T(8,128)S(1)} %fusion.54), kind=kOutput, calls=%fused_computation.20 | convolution fusion | flops 1611268096 | bytes 2099200 | tf_op jit(solution)/shard_map/dot_general | solution.py:19
  32.3 2.0 %fusion.25 = bf16[1024,256]{1,0:T(8,128)(2,1)S(1)} fusion(f32[1024,256]{1,0:T(8,128)S(1)} %fusion.6, f32[1024,256]{1,0:T(8,128)S(1)} %fusion.8, f32[1024,256]{1,0:T(8,128)S(1)} %fusion.10, s32[512]{0:T(512)S(1)} %get-tuple-element.5, f32[512,256]{1,0:T(8,128)S(1)} %fusion.4, f32[512,256]{1,0:T(8,128)S(1)} %fusion.57), kind=kOutput, calls=%fused_computation.37 | convolution fusion | flops 1612316672 | bytes 4720640 | tf_op jit(solution)/shard_map/dot_general | solution.py:19
  34.3 0.8 copy-done.9
  35.1 1.8 %fusion.61 = f32[1024,512]{1,0:T(8,128)} fusion(bf16[1024,256]{1,0:T(8,128)(2,1)S(1)} %fusion.25, bf16[256,512]{1,0:T(8,128)(2,1)S(1)} %copy-done), kind=kOutput, calls=%fused_computation.85 | convolution fusion | flops 268435456 | bytes 2883584 | tf_op jit(solution)/shard_map/dot_general | solution.py:65
  37.1 7.3 %reduce-scatter.2.cloned.1.call-done = f32[1024,256]{1,0:T(8,128)} async-done(((f32[1024,512]{1,0:T(8,128)}), f32[1024,256]{1,0:T(8,128)}) %reduce-scatter.2.cloned.1.call-update) | async-done | bytes 1048592 | tf_op jit(solution)/shard_map/reduce_scatter | solution.py:66
  44.4 2.5 %multiply_convert_fusion = bf16[1024,256]{1,0:T(8,128)(2,1)} fusion(f32[1024,256]{1,0:T(8,128)} %reduce-scatter.2.cloned.1.call-done, bf16[1024,256]{1,0:T(8,128)(2,1)} %param.12), kind=kLoop, calls=%fused_computation.45 | loop fusion | flops 2621440 | bytes 2097152 | tf_op jit(solution)/shard_map/convert_element_type | solution.py:67
  47.0 10.3 %all-gather.2.cloned.1.call-done = bf16[1024,512]{1,0:T(8,128)(2,1)} async-done(((bf16[1024,256]{1,0:T(8,128)(2,1)}), bf16[1024,512]{1,0:T(8,128)(2,1)}) %all-gather.2.cloned.1.call-update) | async-done | bytes 1048592 | tf_op jit(solution)/shard_map/all_gather | solution.py:68
  57.3 1.7 fusion.62
  59.0 1.2 fusion.5
  60.3 1.2 fusion.7
  61.5 1.2 fusion.9
  62.7 1.2 fusion.11
  64.2 2.4 %fusion.3 = f32[1280,256]{1,0:T(8,128)S(1)} fusion(s32[512]{0:T(512)S(1)} %get-tuple-element.10, f32[512,256]{1,0:T(8,128)S(1)} %fusion.11, f32[512,256]{1,0:T(8,128)S(1)} %fusion.57), kind=kOutput, calls=%fused_computation.10 | convolution fusion | flops 2014052352 | bytes 2361344 | tf_op jit(solution)/shard_map/dot_general | solution.py:19
  66.7 2.4 %convolution_add_fusion.2 = f32[1280,256]{1,0:T(8,128)S(1)} fusion(f32[1280,256]{1,0:T(8,128)S(1)} %fusion.3, s32[512]{0:T(512)S(1)} %get-tuple-element.9, f32[512,256]{1,0:T(8,128)S(1)} %fusion.9, f32[512,256]{1,0:T(8,128)S(1)} %fusion.54), kind=kOutput, calls=%fused_computation.2 | convolution fusion | flops 2014380032 | bytes 3672064 | tf_op jit(solution)/shard_map/dot_general | solution.py:19
  69.3 2.6 %convolution_add_fusion.1 = f32[1280,256]{1,0:T(8,128)S(1)} fusion(f32[1280,256]{1,0:T(8,128)S(1)} %convolution_add_fusion.2, s32[512]{0:T(512)S(1)} %get-tuple-element.12, f32[512,256]{1,0:T(8,128)S(1)} %fusion.7, f32[512,256]{1,0:T(8,128)S(1)} %fusion.51), kind=kOutput, calls=%fused_computation.1 | convolution fusion | flops 2014380032 | bytes 3672064 | tf_op jit(solution)/shard_map/dot_general | solution.py:19
  72.0 2.4 %convolution_add_fusion = f32[1280,256]{1,0:T(8,128)S(1)} fusion(f32[1280,256]{1,0:T(8,128)S(1)} %convolution_add_fusion.1, s32[512]{0:T(512)S(1)} %get-tuple-element.11, f32[512,256]{1,0:T(8,128)S(1)} %fusion.5, f32[512,256]{1,0:T(8,128)S(1)} %fusion.48), kind=kOutput, calls=%fused_computation | convolution fusion | flops 2014380032 | bytes 3672064 | tf_op jit(solution)/shard_map/dot_general | solution.py:19
  74.4 0.7 slice.69
  75.1 5.8 %all-to-all-start.1 = ((f32[8,32,256]{2,1,0:T(8,128)}), f32[8,32,256]{2,1,0:T(8,128)}, u32[]{:S(2)}, u32[]{:S(2)}) async-start(f32[8,32,256]{2,1,0:T(8,128)} %bitcast.23), calls=%async_computation.2 | async-start | bytes 524288 | tf_op jit(solution)/shard_map/all_to_all | solution.py:95
  80.9 2.5 %convolution_multiply_fusion = f32[256,512]{1,0:T(8,128)} fusion(bf16[1024,256]{1,0:T(8,128)(2,1)S(1)} %copy-done.10, bf16[1024,512]{1,0:T(8,128)(2,1)} %all-gather.2.cloned.1.call-done), kind=kOutput, calls=%fused_computation.38 | convolution fusion | flops 268566528 | bytes 2097152 | tf_op jit(solution)/shard_map/dot_general | solution.py:69
  83.4 0.8 fusion.27
  84.3 6.1 %all-to-all-done.1 = f32[8,32,256]{2,1,0:T(8,128)} async-done(((f32[8,32,256]{2,1,0:T(8,128)}), f32[8,32,256]{2,1,0:T(8,128)}, u32[]{:S(2)}, u32[]{:S(2)}) %all-to-all-start.1) | async-done | bytes 262176 | tf_op jit(solution)/shard_map/all_to_all | solution.py:95
  90.3 2.8 %fusion.24 = bf16[1024,256]{1,0:T(8,128)(2,1)} fusion(f32[256,256]{1,0:T(8,128)} %bitcast.4, f32[1280,256]{1,0:T(8,128)S(1)} %convolution_add_fusion, s32[256]{0:T(256)S(1)} %bitcast.29), kind=kOutput, calls=%fused_computation.36 | convolution fusion | flops 806092800 | bytes 1836032 | tf_op jit(solution)/shard_map/dot_general | solution.py:19
  93.2 67.4 %all-reduce.3.cloned.1.call-done = (f32[256,512]{1,0:T(8,128)}, f32[64,256]{1,0:T(8,128)}) async-done(((f32[256,512]{1,0:T(8,128)}, f32[64,256]{1,0:T(8,128)}), (f32[256,512]{1,0:T(8,128)}, f32[64,256]{1,0:T(8,128)})) %all-reduce.3.cloned.1.call-update) | async-done | bytes 589840 | tf_op jit(solution)/shard_map/psum | solution.py:93
  160.5 1.9 %copy.13 = f32[256,512]{1,0:T(8,128)} copy(f32[256,512]{1,0:T(8,128)} %get-tuple-element.14) | data formatting | bytes 1048576
  162.4 1.5 copy.14
  (52 shorter events, 3.9 us)
Async XLA Ops:
  7.2 27.9 %copy-start = (bf16[256,512]{1,0:T(8,128)(2,1)S(1)}, bf16[256,512]{1,0:T(8,128)(2,1)}, u32[]{:S(2)}) copy-start(bf16[256,512]{1,0:T(8,128)(2,1)} %param.11) | copy-start | bytes 786436
  7.2 16.8 %copy-start.16 = (bf16[1024,256]{1,0:T(8,128)(2,1)S(1)}, bf16[1024,256]{1,0:T(8,128)(2,1)}, u32[]{:S(2)}) copy-start(bf16[1024,256]{1,0:T(8,128)(2,1)} %param.8) | copy-start | bytes 1572868
  7.2 11.7 %copy-start.11 = (bf16[64,2048]{1,0:T(8,128)(2,1)S(1)}, bf16[64,2048]{1,0:T(8,128)(2,1)}, u32[]{:S(2)}) copy-start(bf16[64,2048]{1,0:T(8,128)(2,1)} %param.9) | copy-start | bytes 786436
  7.2 11.7 %copy-start.12 = (bf16[64,256]{1,0:T(8,128)(2,1)S(1)}, bf16[64,256]{1,0:T(8,128)(2,1)}, u32[]{:S(2)}) copy-start(bf16[64,256]{1,0:T(8,128)(2,1)} %param.10) | copy-start | bytes 98308
  7.2 12.2 %copy-start.13 = (s32[2048]{0:T(1024)S(1)}, s32[2048]{0:T(1024)}, u32[]{:S(2)}) copy-start(s32[2048]{0:T(1024)} %param.14) | copy-start | bytes 24580
  7.2 12.2 %copy-start.14 = (s32[2048]{0:T(1024)S(1)}, s32[2048]{0:T(1024)}, u32[]{:S(2)}) copy-start(s32[2048]{0:T(1024)} %param.15) | copy-start | bytes 24580
  9.4 14.6 %all-to-all-start = ((bf16[8,32,256]{2,1,0:T(8,128)(2,1)}), bf16[8,32,256]{2,1,0:T(8,128)(2,1)S(1)}, u32[]{:S(2)}, u32[]{:S(2)}) async-start(bf16[8,32,256]{2,1,0:T(8,128)(2,1)} %bitcast.1), calls=%async_computation | async-start | bytes 262144 | tf_op jit(solution)/shard_map/all_to_all | solution.py:40
  16.6 27.8 %reduce-scatter.2.cloned.1.call-start = ((), (), s32[]{:S(2)}) async-start(), calls=%async_computation.3 | async-start | bytes 3145728 | tf_op jit(solution)/shard_map/reduce_scatter | solution.py:66
  24.0 1.2 copy-start.17
  24.6 5.7 %copy-start.3 = (f32[512,256]{1,0:T(8,128)}, f32[512,256]{1,0:T(8,128)S(1)}, u32[]{:S(2)}) copy-start(f32[512,256]{1,0:T(8,128)S(1)} %fusion.2) | copy-start | bytes 1572868
  25.2 1.2 copy-start.1
  26.4 5.8 %copy-start.5 = (f32[512,256]{1,0:T(8,128)}, f32[512,256]{1,0:T(8,128)S(1)}, u32[]{:S(2)}) copy-start(f32[512,256]{1,0:T(8,128)S(1)} %fusion.4) | copy-start | bytes 1572868
  34.3 0.8 copy-start.9
  36.9 20.5 %all-gather.2.cloned.1.call-start = ((), (), s32[]{:S(2)}) async-start(), calls=%async_computation.4 | async-start | bytes 1572864 | tf_op jit(solution)/shard_map/all_gather | solution.py:68
  60.3 11.7 %copy-start.7 = (f32[512,256]{1,0:T(8,128)}, f32[512,256]{1,0:T(8,128)S(1)}, u32[]{:S(2)}) copy-start(f32[512,256]{1,0:T(8,128)S(1)} %fusion.5) | copy-start | bytes 1572868
  61.5 2.5 %copy-start.6 = (f32[512,256]{1,0:T(8,128)S(1)}, f32[512,256]{1,0:T(8,128)}, u32[]{:S(2)}) copy-start(f32[512,256]{1,0:T(8,128)} %copy-done.5) | copy-start | bytes 1572868
  64.0 2.6 %copy-start.4 = (f32[512,256]{1,0:T(8,128)S(1)}, f32[512,256]{1,0:T(8,128)}, u32[]{:S(2)}) copy-start(f32[512,256]{1,0:T(8,128)} %copy-done.3) | copy-start | bytes 1572868
  66.7 2.4 %copy-start.2 = (f32[512,256]{1,0:T(8,128)S(1)}, f32[512,256]{1,0:T(8,128)}, u32[]{:S(2)}) copy-start(f32[512,256]{1,0:T(8,128)} %copy-done.1) | copy-start | bytes 1572868
  72.0 9.0 %copy-start.10 = (bf16[1024,256]{1,0:T(8,128)(2,1)S(1)}, bf16[1024,256]{1,0:T(8,128)(2,1)}, u32[]{:S(2)}) copy-start(bf16[1024,256]{1,0:T(8,128)(2,1)} %copy-done.9) | copy-start | bytes 1572868
  74.4 9.1 %copy-start.8 = (f32[512,256]{1,0:T(8,128)S(1)}, f32[512,256]{1,0:T(8,128)}, u32[]{:S(2)}) copy-start(f32[512,256]{1,0:T(8,128)} %copy-done.7) | copy-start | bytes 1572868
  75.1 15.2 %all-to-all-start.1 = ((f32[8,32,256]{2,1,0:T(8,128)}), f32[8,32,256]{2,1,0:T(8,128)}, u32[]{:S(2)}, u32[]{:S(2)}) async-start(f32[8,32,256]{2,1,0:T(8,128)} %bitcast.23), calls=%async_computation.2 | async-start | bytes 524288 | tf_op jit(solution)/shard_map/all_to_all | solution.py:95
  80.9 9.4 %copy-start.15 = (s32[1,256]{1,0:T(1,128)S(1)}, s32[1,256]{1,0:T(1,128)}, u32[]{:S(2)}) copy-start(s32[1,256]{1,0:T(1,128)} %param.13) | copy-start | bytes 3076
  80.9 79.6 %all-reduce.3.cloned.1.call-start = ((), (), s32[]{:S(2)}) async-start(), calls=%async_computation.5 | async-start | bytes 1179648 | tf_op jit(solution)/shard_map/psum | solution.py:93
Sparse Core Ops, SparseCore 0:
  37.0 7.3 reduce-scatter.1
  47.1 10.1 all-gather.1
  86.1 74.4 all-reduce.2
where the time goes:
time: 171 us; the launch traced here: 170 us
  waiting for transfers between devices  95.7 us (56%)
  matrix products  39.7 us (23%)
  between operations  14.2 us (8%)
  starting transfers between devices  13.4 us (8%)
  local copies, waits for them, and re-layouts  4.93 us (3%)
  other arithmetic  2.54 us (1%)
    psum x1, waiting for transfers between devices, on_device(): lax.psum((grad_up_local, grad_basis_local), 'graph')  67.4 us
    dot_general x9, matrix products, spread_sum(): lax.dot_general(select, values, (((0,), (0,)), ((), ())), precision=lax.P...  20.3 us
    all_gather x1, waiting for transfers between devices, on_device(): g_pre = lax.all_gather(g_half, 'mp', axis=1, tiled=True)  10.3 us
    reduce_scatter x1, waiting for transfers between devices, on_device(): pre = lax.psum_scatter(partial_value, 'mp', scatter_dimension=1, tiled=True)  7.33 us
    all_to_all x1, starting transfers between devices, on_device(): lax.all_to_all(packed.reshape(n_graph, capacity, half_width), 'graph', sp...  7.25 us
    all_to_all x1, waiting for transfers between devices, on_device(): lax.all_to_all(outgoing, 'graph', split_axis=0, concat_axis=0, tiled=True)  6.06 us
    all_to_all x1, starting transfers between devices, on_device(): lax.all_to_all(outgoing, 'graph', split_axis=0, concat_axis=0, tiled=True)  5.8 us
    dot_general x4, matrix products, on_device(): jnp.dot(one_hot(outs, local_rows, jnp.float32), g_agg, precision=lax.Prec...  4.87 us
  transfers between devices with their start and end apart: 5, of which 5 were waited for; matrix products, arithmetic and copies ran while one was open for 5% of the time, Pallas kernels for 0%

commit v1 on v0

v1 whole, which is shorter than its diff:
```python
import functools

import jax
import jax.numpy as jnp
from jax import lax
from jax.experimental import pallas as pl
from jax.experimental.pallas import tpu as pltpu
from jax.sharding import PartitionSpec as P

BF16 = jnp.bfloat16
F32 = jnp.float32
LANES = 128
BLOCK = 512
VMEM_LIMIT = 16 * 1024 * 1024


def as_column(row):
    return jnp.broadcast_to(row, (LANES, LANES)).T


def select_rows(index_ref, first, length, count, base):
    wide = lax.broadcasted_iota(jnp.int32, (LANES, count), 1) + base
    parts = []
    for at in range(first // LANES, (first + length) // LANES):
        column = as_column(index_ref[at : at + 1, :])
        parts.append(jnp.where(jnp.tile(column, (1, count // LANES)) == wide, 1.0, 0.0).astype(BF16))
    return jnp.concatenate(parts, axis=0)


def select_columns(index_ref, first, length, count, base):
    tall = lax.broadcasted_iota(jnp.int32, (count, LANES), 0) + base
    parts = []
    for at in range(first // LANES, (first + length) // LANES):
        parts.append(jnp.where(index_ref[at : at + 1, :] == tall, 1.0, 0.0).astype(BF16))
    return jnp.concatenate(parts, axis=1)


def dot(a, b):
    return jnp.dot(a, b, preferred_element_type=F32)


def dot_tn(a, b):
    return lax.dot_general(a, b, (((0,), (0,)), ((), ())), preferred_element_type=F32)


def dot_nt(a, b):
    return lax.dot_general(a, b, (((1,), (1,)), ((), ())), preferred_element_type=F32)


def pack_kernel(send_ref, edges_ref, out_ref):
    rows = out_ref.shape[0]
    step = min(rows, BLOCK)
    for at in range(0, rows, step):
        select = select_rows(send_ref, at, step, edges_ref.shape[0], 0)
        out_ref[at : at + step, :] = dot(select, edges_ref[...]).astype(BF16)


def near_kernel(slot_ref, edges_ref, out_ref):
    for at in range(0, out_ref.shape[0], BLOCK):
        select = select_rows(slot_ref, at, BLOCK, edges_ref.shape[0], 0)
        out_ref[at : at + BLOCK, :] = dot(select, edges_ref[...]).astype(BF16)


def agg_kernel(slot_ref, out_index_ref, recv_ref, near_ref, basis_ref, wb_ref, rows_ref, agg_ref, msg_ref):
    trips, width = near_ref.shape
    edge_rows = agg_ref.shape[0]
    for at in range(0, trips, BLOCK):
        select = select_rows(slot_ref, at, BLOCK, recv_ref.shape[0], edge_rows)
        row = near_ref[at : at + BLOCK, :].astype(F32) + dot(select, recv_ref[...])
        rows_ref[at : at + BLOCK, :] = row.astype(BF16)
        message = row * dot_tn(basis_ref[:, at : at + BLOCK], wb_ref[...])
        top = message.astype(BF16)
        msg_ref[at : at + BLOCK, :width] = top
        msg_ref[at : at + BLOCK, width:] = (message - top.astype(F32)).astype(BF16)
    half = edge_rows // 2
    for top in range(0, edge_rows, half):
        select = select_columns(out_index_ref, 0, trips, half, top)
        both = dot(select, msg_ref[...])
        agg_ref[top : top + half, :] = (both[:, :width] + both[:, width:]).astype(BF16)


def slope_kernel(where_ref, own_ref, other_ref, w_own_ref, w_other_ref, cot_own_ref, cot_other_ref,
                 keep_ref, send_ref, g_ref):
    rows, half = own_ref.shape
    side = where_ref[0]
    bit = where_ref[1]
    quarter = half // 2
    for which, cot_ref in ((0, cot_own_ref), (1, cot_other_ref)):
        here = pl.multiple_of((side if which == 0 else 1 - side) * half, half)
        columns = pl.ds(here, half)
        pre = dot(own_ref[...], w_own_ref[:, columns]) + dot(other_ref[...], w_other_ref[:, columns])
        sig = 0.5 * jnp.tanh(0.5 * pre) + 0.5
        g = cot_ref[...].astype(F32) * sig * (1.0 + pre * (1.0 - sig))
        g_ref[:, columns] = g.astype(BF16)
    g = g_ref[...]
    kept = own_ref[:, pl.ds(pl.multiple_of(bit * quarter, quarter), quarter)]
    sent = own_ref[:, pl.ds(pl.multiple_of((1 - bit) * quarter, quarter), quarter)]
    for cols, ref in ((sent, send_ref), (kept, keep_ref)):
        part = dot_tn(cols, g).astype(ref.dtype)
        ref[:quarter, :] = part[:, :half]
        ref[quarter:, :] = part[:, half:]


def spread_kernel(slot_ref, out_index_ref, g_ref, w_ref, rows_ref, basis_ref, wb_ref, flow_ref, ret_ref, gb_ref, g_agg_ref):
    trips = rows_ref.shape[0]
    edge_rows = g_ref.shape[0]
    g_agg_ref[...] = dot_nt(g_ref[...], w_ref[...]).astype(BF16)
    total = jnp.zeros(gb_ref.shape, F32)
    for at in range(0, trips, BLOCK):
        select = select_rows(out_index_ref, at, BLOCK, edge_rows, 0)
        g_y = dot(select, g_agg_ref[...])
        flow_ref[at : at + BLOCK, :] = (g_y * dot_tn(basis_ref[:, at : at + BLOCK], wb_ref[...])).astype(BF16)
        tgrad = (g_y * rows_ref[at : at + BLOCK, :].astype(F32)).astype(BF16)
        total = total + dot(basis_ref[:, at : at + BLOCK], tgrad)
    gb_ref[...] = total.astype(BF16)
    step = min(ret_ref.shape[0], 256)
    for top in range(0, ret_ref.shape[0], step):
        select = select_columns(slot_ref, 0, trips, step, edge_rows + top)
        ret_ref[top : top + step, :] = dot(select, flow_ref[...]).astype(BF16)


def finish_kernel(up_scale, basis_scale, where_ref, mine_ref, theirs_ref, up_ref, basis_ref):
    half = up_ref.shape[0]
    quarter = half // 2
    bit = where_ref[1]
    for spot, ref in ((bit, mine_ref), (1 - bit, theirs_ref)):
        rows = pl.ds(pl.multiple_of(spot * quarter, quarter), quarter)
        up_ref[rows, :half] = ref[:quarter, :].astype(F32) * up_scale
        up_ref[rows, half:] = ref[quarter:half, :].astype(F32) * up_scale
    basis_ref[...] = (mine_ref[half:, :].astype(F32) + theirs_ref[half:, :].astype(F32)) * basis_scale


def home_kernel(slot_ref, flow_ref, out_ref):
    rows = out_ref.shape[0]
    half = rows // 2
    for top in range(0, rows, half):
        select = select_columns(slot_ref, 0, flow_ref.shape[0], half, top)
        out_ref[top : top + half, :] = dot(select, flow_ref[...])


def back_kernel(send_ref, returned_ref, home_ref, out_ref):
    select = select_columns(send_ref, 0, returned_ref.shape[0], out_ref.shape[0], 0)
    out_ref[...] = (home_ref[...] + dot(select, returned_ref[...])).astype(BF16)


def call(kernel, outs, flops, *operands, scalars=0, scratch=(), name=None):
    whole = pl.BlockSpec(memory_space=pltpu.VMEM)
    scalar = pl.BlockSpec(memory_space=pltpu.SMEM)
    moved = sum(x.size * x.dtype.itemsize for x in operands) + sum(x.size * x.dtype.itemsize for x in outs)
    return pl.pallas_call(
        kernel,
        out_shape=outs,
        in_specs=[scalar if i < scalars else whole for i in range(len(operands))],
        out_specs=[whole] * len(outs),
        scratch_shapes=scratch,
        compiler_params=pltpu.CompilerParams(vmem_limit_bytes=VMEM_LIMIT),
        cost_estimate=pl.CostEstimate(flops=flops, bytes_accessed=moved, transcendentals=0),
        name=name,
    )(*operands)


def shape(rows, columns, dtype):
    return jax.ShapeDtypeStruct((rows, columns), dtype)


def bit_order(bits, core):
    return [(core + k) % bits for k in range(bits)]


def swap(values, n_graph, step):
    bits = n_graph.bit_length() - 1
    pairs = []
    for g in range(n_graph):
        for core in range(2):
            bit = bit_order(bits, core)[step]
            pairs.append((g * 2 + core, (g ^ (1 << bit)) * 2 + core))
    return lax.ppermute(values, ("graph", "mp"), pairs)


def plus(a, b):
    return a.astype(F32) + b.astype(F32)


def on_device(edges, basis, w_basis, w_up, out_grad, send_index, trip_slot, trip_out):
    n_graph = lax.axis_size("graph")
    bits = n_graph.bit_length() - 1
    edge_rows, half = edges.shape
    packed_rows = send_index.shape[1]
    capacity = packed_rows // n_graph
    trips = basis.shape[1]
    quarter = half // 2
    core = lax.axis_index("mp")
    first_bit = (lax.axis_index("graph") >> jnp.where(core == 0, 0, 1 % bits)) & 1
    place = jnp.stack([core, first_bit]).astype(jnp.int32)
    send = send_index.reshape(packed_rows // LANES, LANES)
    slots = trip_slot.reshape(trips // LANES, LANES)
    outs = trip_out.reshape(trips // LANES, LANES)

    (packed,) = call(pack_kernel, [shape(packed_rows, half, BF16)], 2 * packed_rows * edge_rows * half, send, edges, name="pack")
    received = lax.all_to_all(packed, "graph", 0, 0, tiled=True)
    w_other, cot_other = lax.ppermute((w_up, out_grad), "mp", [(0, 1), (1, 0)])
    (near,) = call(near_kernel, [shape(trips, half, BF16)], 0, slots, edges, name="near")
    rows, agg = call(
        agg_kernel,
        [shape(trips, half, BF16), shape(edge_rows, half, BF16)],
        2 * trips * (packed_rows + 2 * edge_rows) * half,
        slots, outs, received, near, basis, w_basis,
        scratch=[pltpu.VMEM((trips, 2 * half), BF16)],
        name="agg",
    )
    agg_other = lax.ppermute(agg, "mp", [(0, 1), (1, 0)])
    keep, sent, g = call(
        slope_kernel,
        [shape(half, half, F32), shape(half, half, BF16), shape(edge_rows, 2 * half, BF16)],
        12 * edge_rows * half * half,
        place, agg, agg_other, w_up, w_other, out_grad, cot_other,
        scalars=1,
        name="slope",
    )
    got = swap(sent, n_graph, 0)
    flow, leaving, gb = call(
        spread_kernel,
        [shape(trips, half, BF16), shape(packed_rows, half, BF16), shape(basis.shape[0], half, BF16)],
        2 * trips * (edge_rows + packed_rows) * half,
        slots, outs, g, w_up, rows, basis, w_basis,
        scratch=[pltpu.VMEM((edge_rows, half), BF16)],
        name="spread",
    )
    returned = lax.all_to_all(leaving, "graph", 0, 0, tiled=True)
    (home,) = call(home_kernel, [shape(edge_rows, half, F32)], 2 * trips * edge_rows * half, slots, flow, name="home")
    load = jnp.concatenate([plus(keep, got).astype(BF16), gb], axis=0)
    for step in range(1, bits):
        load = plus(load, swap(load, n_graph, step)).astype(BF16)
    last = swap(load, n_graph, 0)
    grad_w_up, grad_w_basis = call(
        functools.partial(finish_kernel, (edge_rows * n_graph) ** (-0.5), (trips * n_graph) ** (-0.5)),
        [shape(half, 2 * half, F32), shape(basis.shape[0], half, F32)],
        4 * half * half,
        place, load, last,
        scalars=1,
        name="finish",
    )
    (grad_edges,) = call(
        back_kernel, [shape(edge_rows, half, BF16)], 2 * packed_rows * edge_rows * half, send, returned, home, name="back"
    )
    return (grad_edges, grad_w_up, grad_w_basis)


def solution(mesh):
    placed = (
        P(("groups", "graph"), "mp"),
        P(None, ("groups", "graph")),
        P(None, "mp"),
        P("mp", None),
        P(("groups", "graph"), "mp"),
        P(("groups", "graph"), None),
        P(("groups", "graph")),
        P(("groups", "graph")),
    )
    return jax.shard_map(
        on_device,
        mesh=mesh,
        in_specs=placed,
        out_specs=(P(("groups", "graph"), "mp"), P(("groups", "mp"), None), P("groups", "mp")),
        check_vma=False,
    )
```

time: 171 us -> 54 us (0.32)
  waiting for transfers between devices: 95.7 us -> 20.2 us
  matrix products: 39.7 us -> 0 us
  Pallas kernels: 0 us -> 15.2 us
  between operations: 14.2 us -> 0.77 us
  other arithmetic: 2.54 us -> 0.21 us
  local copies, waits for them, and re-layouts: 4.93 us -> 2.75 us
    psum x1 -> x0, waiting for transfers between devices: 67.4 us -> none  [on_device(): lax.psum((grad_up_local, grad_basis_local), 'graph')]
    dot_general x29 -> x0, matrix products: 39.7 us -> none  [the longest x9 20.3 us: spread_sum(): lax.dot_general(select, values, (((0,), (0,)), ((), ())), precision=lax.P...]
    pallas_call x0 -> x8, Pallas kernels: none -> 15.2 us  [call(): pl.pallas_call(kernel, out_shape=outs, in_specs=[scalar if i < scalars el...]
    ppermute x0 -> x7, waiting for transfers between devices: none -> 11 us  [the longest x4 9.33 us: swap(): return lax.ppermute(values, ('graph', 'mp'), pairs)]
    all_gather x1 -> x0, waiting for transfers between devices: 10.3 us -> none  [on_device(): g_pre = lax.all_gather(g_half, 'mp', axis=1, tiled=True)]
    reduce_scatter x1 -> x0, waiting for transfers between devices: 7.33 us -> none  [on_device(): pre = lax.psum_scatter(partial_value, 'mp', scatter_dimension=1, tiled=True)]
    ppermute x0 -> x7, starting transfers between devices: none -> 3.07 us  [the longest x4 2.56 us: swap(): return lax.ppermute(values, ('graph', 'mp'), pairs)]
    convert_element_type x1 -> x3, other arithmetic: 2.54 us -> 0.12 us  [the longest x2 0.09 us: on_device(): load = plus(load, swap(load, n_graph, step)).astype(BF16)]
  transfers between devices with their start and end apart: 5 -> 9, of which waited for: 5 -> 6; matrix products, arithmetic and copies ran while one was open for 5% -> 0% of each run, Pallas kernels for 0% -> 20%
where the time goes in v1:
time: 54 us; the launch traced here: 53.6 us
  waiting for transfers between devices  20.2 us (37%)
  Pallas kernels  15.2 us (28%)
  starting transfers between devices  14.5 us (27%)
  local copies, waits for them, and re-layouts  2.75 us (5%)
  between operations  0.77 us (1%)
    pallas_call x8, Pallas kernels, call(): pl.pallas_call(kernel, out_shape=outs, in_specs=[scalar if i < scalars el...  15.2 us
    ppermute x4, waiting for transfers between devices, swap(): return lax.ppermute(values, ('graph', 'mp'), pairs)  9.33 us
    all_to_all x1, starting transfers between devices, on_device(): received = lax.all_to_all(packed, 'graph', 0, 0, tiled=True)  7.38 us
    all_to_all x1, waiting for transfers between devices, on_device(): received = lax.all_to_all(packed, 'graph', 0, 0, tiled=True)  5.98 us
    all_to_all x1, starting transfers between devices, on_device(): returned = lax.all_to_all(leaving, 'graph', 0, 0, tiled=True)  4.03 us
    all_to_all x1, waiting for transfers between devices, on_device(): returned = lax.all_to_all(leaving, 'graph', 0, 0, tiled=True)  3.2 us
    unnamed x22, local copies, waits for them, and re-layouts  2.75 us
    ppermute x4, starting transfers between devices, swap(): return lax.ppermute(values, ('graph', 'mp'), pairs)  2.56 us
  transfers between devices with their start and end apart: 9, of which 6 were waited for; matrix products, arithmetic and copies ran while one was open for 0% of the time, Pallas kernels for 20%

profile of v1, /device:TPU:0, one launch (start us, length us, event | category | flops | bytes accessed | tf_op | source)
XLA Modules:
  0.0 53.6 jit_solution(5335057035931117925)
XLA Ops:
  0.6 0.7 %copy-done.3 = s32[1,256]{1,0:T(1,128)S(1)} copy-done((s32[1,256]{1,0:T(1,128)S(1)}, s32[1,256]{1,0:T(1,128)}, u32[]{:S(2)}) %copy-start.3) | copy-done | bytes 1048
  1.3 1.0 %copy-done = bf16[1024,256]{1,0:T(8,128)(2,1)S(1)} copy-done((bf16[1024,256]{1,0:T(8,128)(2,1)S(1)}, bf16[1024,256]{1,0:T(8,128)(2,1)}, u32[]{:S(2)}) %copy-start) | copy-done | bytes 524312
  2.4 1.1 %pack.1 = bf16[256,256]{1,0:T(8,128)(2,1)} custom-call(s32[2,128]{1,0:T(2,128)S(1)} %bitcast.15, bf16[1024,256]{1,0:T(8,128)(2,1)S(1)} %copy-done), custom_call_target="tpu_custom_call" | custom-call | flops 134217728 | bytes 656384 | tf_op jit(solution)/shard_map/pack/pallas_call | solution.py:150
  3.4 7.4 %all-to-all-start = ((bf16[8,32,256]{2,1,0:T(8,128)(2,1)}), bf16[8,32,256]{2,1,0:T(8,128)(2,1)S(1)}, u32[]{:S(2)}, u32[]{:S(2)}) async-start(bf16[8,32,256]{2,1,0:T(8,128)(2,1)} %bitcast.5), calls=%async_computation | async-start | bytes 262144 | tf_op jit(solution)/shard_map/all_to_all | solution.py:200
  10.8 0.0 collective-permute-start.2
  10.8 0.0 copy-start.5
  10.8 0.0 copy-start.7
  10.8 0.0 copy-start.8
  10.9 1.3 %near.1.near_ref = bf16[2048,256]{1,0:T(8,128)(2,1)S(1)} custom-call(s32[16,128]{1,0:T(8,128)S(1)} %bitcast.11, bf16[1024,256]{1,0:T(8,128)(2,1)S(1)} %copy-done.1), custom_call_target="tpu_custom_call" | custom-call | bytes 1581056 | tf_op jit(solution)/shard_map/near/pallas_call | solution.py:150
  12.2 6.0 %all-to-all-done = bf16[8,32,256]{2,1,0:T(8,128)(2,1)S(1)} async-done(((bf16[8,32,256]{2,1,0:T(8,128)(2,1)}), bf16[8,32,256]{2,1,0:T(8,128)(2,1)S(1)}, u32[]{:S(2)}, u32[]{:S(2)}) %all-to-all-start) | async-done | bytes 131104 | tf_op jit(solution)/shard_map/all_to_all | solution.py:200
  18.1 0.0 copy-start.6
  18.2 0.0 copy-start.4
  18.2 3.0 %agg.1 = (bf16[2048,256]{1,0:T(8,128)(2,1)S(1)}, bf16[1024,256]{1,0:T(8,128)(2,1)S(1)}) custom-call(s32[16,128]{1,0:T(8,128)S(1)} %bitcast.12, s32[16,128]{1,0:T(8,128)S(1)} %bitcast.17, bf16[256,256]{1,0:T(8,128)(2,1)S(1)} %bitcast.10, bf16[2048,256]{1,0:T(8,128)(2,1)S(1)} %near.1.near_ref, bf16[64,2048]{1,0:T(8,128)(2,1)S(1)} %copy-done.5, ...), custom_call_target="tpu_custom_call" | custom-call | flops 2415919104 | bytes 3063808 | tf_op jit(solution)/shard_map/agg/pallas_call | solution.py:150
  21.2 1.0 %copy-done.9 = bf16[2048,256]{1,0:T(8,128)(2,1)} copy-done((bf16[2048,256]{1,0:T(8,128)(2,1)}, bf16[2048,256]{1,0:T(8,128)(2,1)S(1)}, u32[]{:S(2)}) %copy-start.9) | copy-done | bytes 1048600
  22.2 0.5 collective-permute-start.1
  22.7 0.1 pad_add_fusion.where_ref
  22.8 1.7 %collective-permute-done.1.w_other_ref = bf16[256,512]{1,0:T(8,128)(2,1)S(1)} collective-permute-done((bf16[256,512]{1,0:T(8,128)(2,1)S(1)}, bf16[256,512]{1,0:T(8,128)(2,1)S(1)}, u32[]{:S(2)}, u32[]{:S(2)}) %collective-permute-start.1) | collective-permute-done | bytes 262176 | tf_op jit(solution)/shard_map/ppermute | solution.py:201
  24.5 2.2 %slope.1 = (f32[256,256]{1,0:T(8,128)S(1)}, bf16[256,256]{1,0:T(8,128)(2,1)S(1)}, bf16[1024,512]{1,0:T(8,128)(2,1)S(1)}) custom-call(s32[2]{0:T(128)S(1)} %pad_add_fusion.where_ref, bf16[1024,256]{1,0:T(8,128)(2,1)S(1)} %get-tuple-element.13.own_ref, bf16[1024,256]{1,0:T(8,128)(2,1)S(1)} %collective-permute-done.other_ref, bf16[256,512]{1,0:T(8,128)(2,1)S(1)} %copy-done.6, ...), custom_call_target="tpu_custom_call" | custom-call | flops 805306368 | bytes 4063240 | tf_op jit(solution)/shard_map/slope/pallas_call | solution.py:150
  26.7 0.3 collective-permute-start.3
  27.0 3.9 %spread.1 = (bf16[2048,256]{1,0:T(8,128)(2,1)S(1)}, bf16[256,256]{1,0:T(8,128)(2,1)}, bf16[64,256]{1,0:T(8,128)(2,1)S(1)}) custom-call(s32[16,128]{1,0:T(8,128)S(1)} %bitcast.13, s32[16,128]{1,0:T(8,128)S(1)} %bitcast.18, bf16[1024,512]{1,0:T(8,128)(2,1)S(1)} %get-tuple-element.14.g_ref, bf16[256,512]{1,0:T(8,128)(2,1)S(1)} %copy-done.6, ...), custom_call_target="tpu_custom_call" | custom-call | flops 1342177280 | bytes 3883008 | tf_op jit(solution)/shard_map/spread/pallas_call | solution.py:150
  30.9 0.9 %collective-permute-done.3 = bf16[256,256]{1,0:T(8,128)(2,1)S(1)} collective-permute-done((bf16[256,256]{1,0:T(8,128)(2,1)S(1)}, bf16[256,256]{1,0:T(8,128)(2,1)S(1)}, u32[]{:S(2)}, u32[]{:S(2)}) %collective-permute-start.3) | collective-permute-done | bytes 131104 | tf_op jit(solution)/shard_map/ppermute | solution.py:177
  31.8 0.3 collective-permute-start.4
  32.1 6.1 %collective-permute-done.4 = bf16[320,256]{1,0:T(8,128)(2,1)S(1)} collective-permute-done((bf16[320,256]{1,0:T(8,128)(2,1)S(1)}, bf16[320,256]{1,0:T(8,128)(2,1)S(1)}, u32[]{:S(2)}, u32[]{:S(2)}) %collective-permute-start.4) | collective-permute-done | bytes 163872 | tf_op jit(solution)/shard_map/ppermute | solution.py:177
  38.2 0.9 %collective-permute-start.5 = (bf16[320,256]{1,0:T(8,128)(2,1)S(1)}, bf16[320,256]{1,0:T(8,128)(2,1)S(1)}, u32[]{:S(2)}, u32[]{:S(2)}) collective-permute-start(bf16[320,256]{1,0:T(8,128)(2,1)S(1)} %add_convert_fusion.1), channel_id=1, source_target_pairs={{0,8},{1,3},{2,10},{3,1},{4,12},{5,7},{6,14},{7,5},{8,0},{9,11},{1... | collective-permute-start | bytes 491528 | tf_op jit(solution)/shard_map/ppermute | solution.py:177
  39.1 4.0 %all-to-all-start.1 = ((bf16[8,32,256]{2,1,0:T(8,128)(2,1)}), bf16[8,32,256]{2,1,0:T(8,128)(2,1)S(1)}, u32[]{:S(2)}, u32[]{:S(2)}) async-start(bf16[8,32,256]{2,1,0:T(8,128)(2,1)} %bitcast.7), calls=%async_computation.1 | async-start | bytes 262144 | tf_op jit(solution)/shard_map/all_to_all | solution.py:229
  43.1 2.4 %collective-permute-done.5 = bf16[320,256]{1,0:T(8,128)(2,1)S(1)} collective-permute-done((bf16[320,256]{1,0:T(8,128)(2,1)S(1)}, bf16[320,256]{1,0:T(8,128)(2,1)S(1)}, u32[]{:S(2)}, u32[]{:S(2)}) %collective-permute-start.5) | collective-permute-done | bytes 163872 | tf_op jit(solution)/shard_map/ppermute | solution.py:177
  45.6 1.1 %collective-permute-start.6 = (bf16[320,256]{1,0:T(8,128)(2,1)S(1)}, bf16[320,256]{1,0:T(8,128)(2,1)S(1)}, u32[]{:S(2)}, u32[]{:S(2)}) collective-permute-start(bf16[320,256]{1,0:T(8,128)(2,1)S(1)} %add_convert_fusion.mine_ref), channel_id=1, source_target_pairs={{0,2},{1,5},{2,0},{3,7},{4,6},{5,1},{6,4},{7,3},{8,10},{9,13},{10,... | collective-permute-start | bytes 491528 | tf_op jit(solution)/shard_map/ppermute | solution.py:177
  46.7 1.2 %home.1.home_ref = f32[1024,256]{1,0:T(8,128)S(1)} custom-call(s32[16,128]{1,0:T(8,128)S(1)} %bitcast.14, bf16[2048,256]{1,0:T(8,128)(2,1)S(1)} %get-tuple-element.17.flow_ref), custom_call_target="tpu_custom_call" | custom-call | flops 1073741824 | bytes 2105344 | tf_op jit(solution)/shard_map/home/pallas_call | solution.py:150
  47.9 3.2 %all-to-all-done.1 = bf16[8,32,256]{2,1,0:T(8,128)(2,1)S(1)} async-done(((bf16[8,32,256]{2,1,0:T(8,128)(2,1)}), bf16[8,32,256]{2,1,0:T(8,128)(2,1)S(1)}, u32[]{:S(2)}, u32[]{:S(2)}) %all-to-all-start.1) | async-done | bytes 131104 | tf_op jit(solution)/shard_map/all_to_all | solution.py:229
  51.1 1.1 %back.1 = bf16[1024,256]{1,0:T(8,128)(2,1)} custom-call(s32[2,128]{1,0:T(2,128)S(1)} %bitcast.16, bf16[256,256]{1,0:T(8,128)(2,1)S(1)} %bitcast.9, f32[1024,256]{1,0:T(8,128)S(1)} %home.1.home_ref), custom_call_target="tpu_custom_call" | custom-call | flops 134217728 | bytes 1704960 | tf_op jit(solution)/shard_map/back/pallas_call | solution.py:150
  52.2 0.0 collective-permute-done.6.theirs_ref
  52.2 1.4 %finish.1 = (f32[256,512]{1,0:T(8,128)}, f32[64,256]{1,0:T(8,128)}) custom-call(s32[2]{0:T(128)S(1)} %pad_add_fusion.where_ref, bf16[320,256]{1,0:T(8,128)(2,1)S(1)} %add_convert_fusion.mine_ref, bf16[320,256]{1,0:T(8,128)(2,1)S(1)} %collective-permute-done.6.theirs_ref), custom_call_target="tpu_custom_call" | custom-call | flops 262144 | bytes 917512 | tf_op jit(solution)/shard_map/finish/pallas_call | solution.py:150
  (21 shorter events, 0.2 us)
Async XLA Ops:
  0.6 0.7 %copy-start.3 = (s32[1,256]{1,0:T(1,128)S(1)}, s32[1,256]{1,0:T(1,128)}, u32[]{:S(2)}) copy-start(s32[1,256]{1,0:T(1,128)} %param.13) | copy-start | bytes 3076
  1.3 1.0 %copy-start = (bf16[1024,256]{1,0:T(8,128)(2,1)S(1)}, bf16[1024,256]{1,0:T(8,128)(2,1)}, u32[]{:S(2)}) copy-start(bf16[1024,256]{1,0:T(8,128)(2,1)} %edges_ref.3) | copy-start | bytes 1572868
  2.4 8.5 %copy-start.1 = (bf16[1024,256]{1,0:T(8,128)(2,1)S(1)}, bf16[1024,256]{1,0:T(8,128)(2,1)}, u32[]{:S(2)}) copy-start(bf16[1024,256]{1,0:T(8,128)(2,1)} %edges_ref.3) | copy-start | bytes 1572868
  3.4 7.4 %copy-start.2 = (s32[2048]{0:T(1024)S(1)}, s32[2048]{0:T(1024)}, u32[]{:S(2)}) copy-start(s32[2048]{0:T(1024)} %param.14) | copy-start | bytes 24580
  3.4 14.7 %all-to-all-start = ((bf16[8,32,256]{2,1,0:T(8,128)(2,1)}), bf16[8,32,256]{2,1,0:T(8,128)(2,1)S(1)}, u32[]{:S(2)}, u32[]{:S(2)}) async-start(bf16[8,32,256]{2,1,0:T(8,128)(2,1)} %bitcast.5), calls=%async_computation | async-start | bytes 262144 | tf_op jit(solution)/shard_map/all_to_all | solution.py:200
  10.8 13.7 %collective-permute-start.2 = (bf16[1024,256]{1,0:T(8,128)(2,1)}, bf16[1024,256]{1,0:T(8,128)(2,1)S(1)}, u32[]{:S(2)}, u32[]{:S(2)}) collective-permute-start(bf16[1024,256]{1,0:T(8,128)(2,1)} %cot_own_ref.1), channel_id=1, source_target_pairs={{0,1},{1,0},{2,3},{3,2},{4,5},{5,4},{6,7},{7,6},{8,9},{9,8},{10,11... | collective-permute-start | bytes 1572872 | tf_op jit(solution)/shard_map/ppermute | solution.py:201
  10.8 7.3 %copy-start.5 = (bf16[64,2048]{1,0:T(8,128)(2,1)S(1)}, bf16[64,2048]{1,0:T(8,128)(2,1)}, u32[]{:S(2)}) copy-start(bf16[64,2048]{1,0:T(8,128)(2,1)} %basis_ref.3) | copy-start | bytes 786436
  10.8 7.3 %copy-start.7 = (bf16[64,256]{1,0:T(8,128)(2,1)S(1)}, bf16[64,256]{1,0:T(8,128)(2,1)}, u32[]{:S(2)}) copy-start(bf16[64,256]{1,0:T(8,128)(2,1)} %wb_ref.3) | copy-start | bytes 98308
  10.8 7.3 %copy-start.8 = (s32[2048]{0:T(1024)S(1)}, s32[2048]{0:T(1024)}, u32[]{:S(2)}) copy-start(s32[2048]{0:T(1024)} %param.15) | copy-start | bytes 24580
  18.1 4.0 %copy-start.6 = (bf16[256,512]{1,0:T(8,128)(2,1)S(1)}, bf16[256,512]{1,0:T(8,128)(2,1)}, u32[]{:S(2)}) copy-start(bf16[256,512]{1,0:T(8,128)(2,1)} %w_ref.1) | copy-start | bytes 786436
  18.2 6.3 %copy-start.4 = (bf16[1024,256]{1,0:T(8,128)(2,1)S(1)}, bf16[1024,256]{1,0:T(8,128)(2,1)}, u32[]{:S(2)}) copy-start(bf16[1024,256]{1,0:T(8,128)(2,1)} %cot_own_ref.1) | copy-start | bytes 1572868
  21.2 1.0 %copy-start.9 = (bf16[2048,256]{1,0:T(8,128)(2,1)}, bf16[2048,256]{1,0:T(8,128)(2,1)S(1)}, u32[]{:S(2)}) copy-start(bf16[2048,256]{1,0:T(8,128)(2,1)S(1)} %get-tuple-element.15.rows_ref) | copy-start | bytes 3145732
  22.2 2.3 %collective-permute-start = (bf16[1024,256]{1,0:T(8,128)(2,1)S(1)}, bf16[1024,256]{1,0:T(8,128)(2,1)S(1)}, u32[]{:S(2)}, u32[]{:S(2)}) collective-permute-start(bf16[1024,256]{1,0:T(8,128)(2,1)S(1)} %get-tuple-element.13.own_ref), channel_id=1, source_target_pairs={{0,1},{1,0},{2,3},{3,2},{4,5},{5,4},{6,7},{7,6},{8,9},{9,8},{10,11... | collective-permute-start | bytes 1572872 | tf_op jit(solution)/shard_map/ppermute | solution.py:211
  22.2 2.3 %collective-permute-start.1 = (bf16[256,512]{1,0:T(8,128)(2,1)S(1)}, bf16[256,512]{1,0:T(8,128)(2,1)S(1)}, u32[]{:S(2)}, u32[]{:S(2)}) collective-permute-start(bf16[256,512]{1,0:T(8,128)(2,1)S(1)} %copy-done.6), channel_id=1, source_target_pairs={{0,1},{1,0},{2,3},{3,2},{4,5},{5,4},{6,7},{7,6},{8,9},{9,8},{10,11... | collective-permute-start | bytes 786440 | tf_op jit(solution)/shard_map/ppermute | solution.py:201
  22.8 4.2 %copy-start.10 = (bf16[2048,256]{1,0:T(8,128)(2,1)S(1)}, bf16[2048,256]{1,0:T(8,128)(2,1)}, u32[]{:S(2)}) copy-start(bf16[2048,256]{1,0:T(8,128)(2,1)} %copy-done.9) | copy-start | bytes 3145732
  26.7 5.0 %collective-permute-start.3 = (bf16[256,256]{1,0:T(8,128)(2,1)S(1)}, bf16[256,256]{1,0:T(8,128)(2,1)S(1)}, u32[]{:S(2)}, u32[]{:S(2)}) collective-permute-start(bf16[256,256]{1,0:T(8,128)(2,1)S(1)} %get-tuple-element.19), channel_id=1, source_target_pairs={{0,2},{1,5},{2,0},{3,7},{4,6},{5,1},{6,4},{7,3},{8,10},{9,13},{10,... | collective-permute-start | bytes 393224 | tf_op jit(solution)/shard_map/ppermute | solution.py:177
  31.8 6.3 %collective-permute-start.4 = (bf16[320,256]{1,0:T(8,128)(2,1)S(1)}, bf16[320,256]{1,0:T(8,128)(2,1)S(1)}, u32[]{:S(2)}, u32[]{:S(2)}) collective-permute-start(bf16[320,256]{1,0:T(8,128)(2,1)S(1)} %pad_maximum_fusion), channel_id=1, source_target_pairs={{0,4},{1,9},{2,6},{3,11},{4,0},{5,13},{6,2},{7,15},{8,12},{9,1},{1... | collective-permute-start | bytes 491528 | tf_op jit(solution)/shard_map/ppermute | solution.py:177
  38.2 7.3 %collective-permute-start.5 = (bf16[320,256]{1,0:T(8,128)(2,1)S(1)}, bf16[320,256]{1,0:T(8,128)(2,1)S(1)}, u32[]{:S(2)}, u32[]{:S(2)}) collective-permute-start(bf16[320,256]{1,0:T(8,128)(2,1)S(1)} %add_convert_fusion.1), channel_id=1, source_target_pairs={{0,8},{1,3},{2,10},{3,1},{4,12},{5,7},{6,14},{7,5},{8,0},{9,11},{1... | collective-permute-start | bytes 491528 | tf_op jit(solution)/shard_map/ppermute | solution.py:177
  39.1 12.0 %all-to-all-start.1 = ((bf16[8,32,256]{2,1,0:T(8,128)(2,1)}), bf16[8,32,256]{2,1,0:T(8,128)(2,1)S(1)}, u32[]{:S(2)}, u32[]{:S(2)}) async-start(bf16[8,32,256]{2,1,0:T(8,128)(2,1)} %bitcast.7), calls=%async_computation.1 | async-start | bytes 262144 | tf_op jit(solution)/shard_map/all_to_all | solution.py:229
  45.6 6.6 %collective-permute-start.6 = (bf16[320,256]{1,0:T(8,128)(2,1)S(1)}, bf16[320,256]{1,0:T(8,128)(2,1)S(1)}, u32[]{:S(2)}, u32[]{:S(2)}) collective-permute-start(bf16[320,256]{1,0:T(8,128)(2,1)S(1)} %add_convert_fusion.mine_ref), channel_id=1, source_target_pairs={{0,2},{1,5},{2,0},{3,7},{4,6},{5,1},{6,4},{7,3},{8,10},{9,13},{10,... | collective-permute-start | bytes 491528 | tf_op jit(solution)/shard_map/ppermute | solution.py:177

commit v2 on v1

--- a/solution.py
+++ b/solution.py
@@ -47,12 +47,9 @@
     return lax.dot_general(a, b, (((1,), (1,)), ((), ())), preferred_element_type=F32)
 
 
-def pack_kernel(send_ref, edges_ref, out_ref):
-    rows = out_ref.shape[0]
-    step = min(rows, BLOCK)
-    for at in range(0, rows, step):
-        select = select_rows(send_ref, at, step, edges_ref.shape[0], 0)
-        out_ref[at : at + step, :] = dot(select, edges_ref[...]).astype(BF16)
+def pack(send_index, edges):
+    rows = jnp.arange(edges.shape[0], dtype=jnp.int32)
+    return dot((send_index[:, None] == rows[None, :]).astype(BF16), edges).astype(BF16)
 
 
 def near_kernel(slot_ref, edges_ref, out_ref):
@@ -79,24 +76,24 @@
         agg_ref[top : top + half, :] = (both[:, :width] + both[:, width:]).astype(BF16)
 
 
-def slope_kernel(where_ref, own_ref, other_ref, w_own_ref, w_other_ref, cot_own_ref, cot_other_ref,
-                 keep_ref, send_ref, g_ref):
-    rows, half = own_ref.shape
+def ready_kernel(own_ref, w_ref, pre_ref, turned_ref):
+    pre_ref[...] = dot(own_ref[...], w_ref[...])
+    turned_ref[...] = own_ref[...].T
+
+
+def slope_kernel(where_ref, pre_ref, turned_ref, other_ref, w_ref, cot_own_ref, cot_other_ref, keep_ref, send_ref, g_ref):
+    half = other_ref.shape[1]
+    quarter = half // 2
     side = where_ref[0]
     bit = where_ref[1]
-    quarter = half // 2
-    for which, cot_ref in ((0, cot_own_ref), (1, cot_other_ref)):
-        here = pl.multiple_of((side if which == 0 else 1 - side) * half, half)
-        columns = pl.ds(here, half)
-        pre = dot(own_ref[...], w_own_ref[:, columns]) + dot(other_ref[...], w_other_ref[:, columns])
+    for spot, cot_ref in ((side, cot_own_ref), (1 - side, cot_other_ref)):
+        columns = pl.ds(pl.multiple_of(spot * half, half), half)
+        pre = pre_ref[:, columns] + dot(other_ref[...], w_ref[:, columns])
         sig = 0.5 * jnp.tanh(0.5 * pre) + 0.5
         g = cot_ref[...].astype(F32) * sig * (1.0 + pre * (1.0 - sig))
         g_ref[:, columns] = g.astype(BF16)
-    g = g_ref[...]
-    kept = own_ref[:, pl.ds(pl.multiple_of(bit * quarter, quarter), quarter)]
-    sent = own_ref[:, pl.ds(pl.multiple_of((1 - bit) * quarter, quarter), quarter)]
-    for cols, ref in ((sent, send_ref), (kept, keep_ref)):
-        part = dot_tn(cols, g).astype(ref.dtype)
+    for spot, ref in ((1 - bit, send_ref), (bit, keep_ref)):
+        part = dot(turned_ref[pl.ds(pl.multiple_of(spot * quarter, quarter), quarter), :], g_ref[...]).astype(ref.dtype)
         ref[:quarter, :] = part[:, :half]
         ref[quarter:, :] = part[:, half:]
 
@@ -119,7 +116,16 @@
         ret_ref[top : top + step, :] = dot(select, flow_ref[...]).astype(BF16)
 
 
-def finish_kernel(up_scale, basis_scale, where_ref, mine_ref, theirs_ref, up_ref, basis_ref):
+def home_kernel(slot_ref, flow_ref, out_ref):
+    rows = out_ref.shape[0]
+    half = rows // 2
+    for top in range(0, rows, half):
+        select = select_columns(slot_ref, 0, flow_ref.shape[0], half, top)
+        out_ref[top : top + half, :] = dot(select, flow_ref[...])
+
+
+def finish_kernel(up_scale, basis_scale, where_ref, send_ref, returned_ref, home_ref, mine_ref, theirs_ref,
+                  edges_ref, up_ref, basis_ref):
     half = up_ref.shape[0]
     quarter = half // 2
     bit = where_ref[1]
@@ -128,19 +134,8 @@
         up_ref[rows, :half] = ref[:quarter, :].astype(F32) * up_scale
         up_ref[rows, half:] = ref[quarter:half, :].astype(F32) * up_scale
     basis_ref[...] = (mine_ref[half:, :].astype(F32) + theirs_ref[half:, :].astype(F32)) * basis_scale
-
-
-def home_kernel(slot_ref, flow_ref, out_ref):
-    rows = out_ref.shape[0]
-    half = rows // 2
-    for top in range(0, rows, half):
-        select = select_columns(slot_ref, 0, flow_ref.shape[0], half, top)
-        out_ref[top : top + half, :] = dot(select, flow_ref[...])
-
-
-def back_kernel(send_ref, returned_ref, home_ref, out_ref):
-    select = select_columns(send_ref, 0, returned_ref.shape[0], out_ref.shape[0], 0)
-    out_ref[...] = (home_ref[...] + dot(select, returned_ref[...])).astype(BF16)
+    select = select_columns(send_ref, 0, returned_ref.shape[0], edges_ref.shape[0], 0)
+    edges_ref[...] = (home_ref[...] + dot(select, returned_ref[...])).astype(BF16)
 
 
 def call(kernel, outs, flops, *operands, scalars=0, scratch=(), name=None):
@@ -196,8 +191,7 @@
     slots = trip_slot.reshape(trips // LANES, LANES)
     outs = trip_out.reshape(trips // LANES, LANES)
 
-    (packed,) = call(pack_kernel, [shape(packed_rows, half, BF16)], 2 * packed_rows * edge_rows * half, send, edges, name="pack")
-    received = lax.all_to_all(packed, "graph", 0, 0, tiled=True)
+    received = lax.all_to_all(pack(send_index[0], edges), "graph", 0, 0, tiled=True)
     w_other, cot_other = lax.ppermute((w_up, out_grad), "mp", [(0, 1), (1, 0)])
     (near,) = call(near_kernel, [shape(trips, half, BF16)], 0, slots, edges, name="near")
     rows, agg = call(
@@ -209,11 +203,18 @@
         name="agg",
     )
     agg_other = lax.ppermute(agg, "mp", [(0, 1), (1, 0)])
+    pre_own, turned = call(
+        ready_kernel,
+        [shape(edge_rows, 2 * half, F32), shape(half, edge_rows, BF16)],
+        4 * edge_rows * half * half,
+        agg, w_up,
+        name="ready",
+    )
     keep, sent, g = call(
         slope_kernel,
         [shape(half, half, F32), shape(half, half, BF16), shape(edge_rows, 2 * half, BF16)],
-        12 * edge_rows * half * half,
-        place, agg, agg_other, w_up, w_other, out_grad, cot_other,
+        8 * edge_rows * half * half,
+        place, pre_own, turned, agg_other, w_other, out_grad, cot_other,
         scalars=1,
         name="slope",
     )
@@ -232,18 +233,14 @@
     for step in range(1, bits):
         load = plus(load, swap(load, n_graph, step)).astype(BF16)
     last = swap(load, n_graph, 0)
-    grad_w_up, grad_w_basis = call(
+    return call(
         functools.partial(finish_kernel, (edge_rows * n_graph) ** (-0.5), (trips * n_graph) ** (-0.5)),
-        [shape(half, 2 * half, F32), shape(basis.shape[0], half, F32)],
-        4 * half * half,
-        place, load, last,
+        [shape(edge_rows, half, BF16), shape(half, 2 * half, F32), shape(basis.shape[0], half, F32)],
+        2 * packed_rows * edge_rows * half,
+        place, send, returned, home, load, last,
         scalars=1,
         name="finish",
     )
-    (grad_edges,) = call(
-        back_kernel, [shape(edge_rows, half, BF16)], 2 * packed_rows * edge_rows * half, send, returned, home, name="back"
-    )
-    return (grad_edges, grad_w_up, grad_w_basis)
 
 
 def solution(mesh):

time: 54 us -> 52.5 us (0.972)
  waiting for transfers between devices: 20.2 us -> 16.8 us
  matrix products: 0 us -> 2.11 us
  Pallas kernels: 15.2 us -> 13.7 us
  local copies, waits for them, and re-layouts: 2.75 us -> 4.01 us
    dot_general x0 -> x1, matrix products: none -> 2.11 us  [dot(): return jnp.dot(a, b, preferred_element_type=F32)]
    all_to_all x1, waiting for transfers between devices: 5.98 us -> 4.29 us  [on_device(): lax.all_to_all(pack(send_index[0], edges), 'graph', 0, 0, tiled=True)]
    pallas_call x8 -> x7, Pallas kernels: 15.2 us -> 13.7 us  [call(): pl.pallas_call(kernel, out_shape=outs, in_specs=[scalar if i < scalars el...]
    unnamed x22 -> x26, local copies, waits for them, and re-layouts: 2.75 us -> 4.01 us
    all_to_all x1, waiting for transfers between devices: 3.2 us -> 1.94 us  [on_device(): returned = lax.all_to_all(leaving, 'graph', 0, 0, tiled=True)]
  transfers between devices with their start and end apart: 9 -> 9, of which waited for: 6 -> 6; matrix products, arithmetic and copies ran while one was open for 0% -> 0% of each run, Pallas kernels for 20% -> 19%
where the time goes in v2:
time: 52.5 us; the launch traced here: 52.1 us
  waiting for transfers between devices  16.8 us (32%)
  starting transfers between devices  14.4 us (27%)
  Pallas kernels  13.7 us (26%)
  local copies, waits for them, and re-layouts  4.01 us (8%)
  matrix products  2.11 us (4%)
  between operations  0.8 us (2%)
    pallas_call x7, Pallas kernels, call(): pl.pallas_call(kernel, out_shape=outs, in_specs=[scalar if i < scalars el...  13.7 us
    ppermute x4, waiting for transfers between devices, swap(): return lax.ppermute(values, ('graph', 'mp'), pairs)  9.35 us
    all_to_all x1, starting transfers between devices, on_device(): lax.all_to_all(pack(send_index[0], edges), 'graph', 0, 0, tiled=True)  7.25 us
    all_to_all x1, waiting for transfers between devices, on_device(): lax.all_to_all(pack(send_index[0], edges), 'graph', 0, 0, tiled=True)  4.29 us
    unnamed x26, local copies, waits for them, and re-layouts  4.01 us
    all_to_all x1, starting transfers between devices, on_device(): returned = lax.all_to_all(leaving, 'graph', 0, 0, tiled=True)  3.96 us
    ppermute x4, starting transfers between devices, swap(): return lax.ppermute(values, ('graph', 'mp'), pairs)  2.67 us
    dot_general x1, matrix products, dot(): return jnp.dot(a, b, preferred_element_type=F32)  2.11 us
  transfers between devices with their start and end apart: 9, of which 6 were waited for; matrix products, arithmetic and copies ran while one was open for 0% of the time, Pallas kernels for 19%

profile of v2, /device:TPU:0, one launch (start us, length us, event | category | flops | bytes accessed | tf_op | source)
XLA Modules:
  0.0 52.1 jit_solution(8358640137346809885)
XLA Ops:
  0.6 0.0 copy-start.3
  0.7 2.1 %convolution_convert_fusion = bf16[256,256]{1,0:T(8,128)(2,1)} fusion(bf16[1024,256]{1,0:T(8,128)(2,1)} %edges_ref.1, s32[256]{0:T(256)} %bitcast.17), kind=kOutput, calls=%fused_computation | convolution fusion | flops 134545408 | bytes 656384 | tf_op jit(solution)/shard_map/dot_general | solution.py:39
  2.8 7.3 %all-to-all-start = ((bf16[8,32,256]{2,1,0:T(8,128)(2,1)}), bf16[8,32,256]{2,1,0:T(8,128)(2,1)S(1)}, u32[]{:S(2)}, u32[]{:S(2)}) async-start(bf16[8,32,256]{2,1,0:T(8,128)(2,1)} %bitcast.6), calls=%async_computation | async-start | bytes 262144 | tf_op jit(solution)/shard_map/all_to_all | solution.py:194
  10.1 0.0 copy-start
  10.1 1.0 %copy-done = bf16[1024,256]{1,0:T(8,128)(2,1)S(1)} copy-done((bf16[1024,256]{1,0:T(8,128)(2,1)S(1)}, bf16[1024,256]{1,0:T(8,128)(2,1)}, u32[]{:S(2)}) %copy-start) | copy-done | bytes 524312
  11.1 0.7 %copy-done.2 = s32[2048]{0:T(1024)S(1)} copy-done((s32[2048]{0:T(1024)S(1)}, s32[2048]{0:T(1024)}, u32[]{:S(2)}) %copy-start.2) | copy-done | bytes 8216
  11.8 1.3 %near.1.near_ref = bf16[2048,256]{1,0:T(8,128)(2,1)S(1)} custom-call(s32[16,128]{1,0:T(8,128)S(1)} %bitcast.13, bf16[1024,256]{1,0:T(8,128)(2,1)S(1)} %copy-done), custom_call_target="tpu_custom_call" | custom-call | bytes 1581056 | tf_op jit(solution)/shard_map/near/pallas_call | solution.py:145
  13.1 4.3 %all-to-all-done = bf16[8,32,256]{2,1,0:T(8,128)(2,1)S(1)} async-done(((bf16[8,32,256]{2,1,0:T(8,128)(2,1)}), bf16[8,32,256]{2,1,0:T(8,128)(2,1)S(1)}, u32[]{:S(2)}, u32[]{:S(2)}) %all-to-all-start) | async-done | bytes 131104 | tf_op jit(solution)/shard_map/all_to_all | solution.py:194
  17.4 0.0 copy-start.6
  17.4 0.0 copy-start.1
  17.4 3.0 %agg.1 = (bf16[2048,256]{1,0:T(8,128)(2,1)S(1)}, bf16[1024,256]{1,0:T(8,128)(2,1)S(1)}) custom-call(s32[16,128]{1,0:T(8,128)S(1)} %bitcast.14, s32[16,128]{1,0:T(8,128)S(1)} %bitcast.19, bf16[256,256]{1,0:T(8,128)(2,1)S(1)} %bitcast.12, bf16[2048,256]{1,0:T(8,128)(2,1)S(1)} %near.1.near_ref, bf16[64,2048]{1,0:T(8,128)(2,1)S(1)} %copy-done.5, ...), custom_call_target="tpu_custom_call" | custom-call | flops 2415919104 | bytes 3063808 | tf_op jit(solution)/shard_map/agg/pallas_call | solution.py:145
  20.4 1.0 %copy-done.11 = bf16[2048,256]{1,0:T(8,128)(2,1)} copy-done((bf16[2048,256]{1,0:T(8,128)(2,1)}, bf16[2048,256]{1,0:T(8,128)(2,1)S(1)}, u32[]{:S(2)}) %copy-start.11) | copy-done | bytes 1048600
  21.5 0.5 collective-permute-start.1
  22.0 0.1 pad_add_fusion.where_ref
  22.0 0.4 ready.1
  22.5 1.3 %collective-permute-done.1.w_ref = bf16[256,512]{1,0:T(8,128)(2,1)S(1)} collective-permute-done((bf16[256,512]{1,0:T(8,128)(2,1)S(1)}, bf16[256,512]{1,0:T(8,128)(2,1)S(1)}, u32[]{:S(2)}, u32[]{:S(2)}) %collective-permute-start.1) | collective-permute-done | bytes 262176 | tf_op jit(solution)/shard_map/ppermute | solution.py:195
  23.8 2.0 %slope.1 = (f32[256,256]{1,0:T(8,128)S(1)}, bf16[256,256]{1,0:T(8,128)(2,1)S(1)}, bf16[1024,512]{1,0:T(8,128)(2,1)S(1)}) custom-call(s32[2]{0:T(128)S(1)} %pad_add_fusion.where_ref, f32[1024,512]{1,0:T(8,128)S(1)} %get-tuple-element.14.pre_ref, bf16[256,1024]{1,0:T(8,128)(2,1)S(1)} %get-tuple-element.15.turned_ref, ...), custom_call_target="tpu_custom_call" | custom-call | flops 536870912 | bytes 5898248 | tf_op jit(solution)/shard_map/slope/pallas_call | solution.py:145
  25.8 0.3 collective-permute-start.3
  26.1 3.9 %spread.1 = (bf16[2048,256]{1,0:T(8,128)(2,1)S(1)}, bf16[256,256]{1,0:T(8,128)(2,1)}, bf16[64,256]{1,0:T(8,128)(2,1)S(1)}) custom-call(s32[16,128]{1,0:T(8,128)S(1)} %bitcast.15, s32[16,128]{1,0:T(8,128)S(1)} %bitcast.20, bf16[1024,512]{1,0:T(8,128)(2,1)S(1)} %get-tuple-element.16.g_ref, bf16[256,512]{1,0:T(8,128)(2,1)S(1)} %copy-done.6, ...), custom_call_target="tpu_custom_call" | custom-call | flops 1342177280 | bytes 3883008 | tf_op jit(solution)/shard_map/spread/pallas_call | solution.py:145
  30.0 0.9 %collective-permute-done.3 = bf16[256,256]{1,0:T(8,128)(2,1)S(1)} collective-permute-done((bf16[256,256]{1,0:T(8,128)(2,1)S(1)}, bf16[256,256]{1,0:T(8,128)(2,1)S(1)}, u32[]{:S(2)}, u32[]{:S(2)}) %collective-permute-start.3) | collective-permute-done | bytes 131104 | tf_op jit(solution)/shard_map/ppermute | solution.py:172
  30.9 0.3 collective-permute-start.4
  31.2 6.1 %collective-permute-done.4 = bf16[320,256]{1,0:T(8,128)(2,1)S(1)} collective-permute-done((bf16[320,256]{1,0:T(8,128)(2,1)S(1)}, bf16[320,256]{1,0:T(8,128)(2,1)S(1)}, u32[]{:S(2)}, u32[]{:S(2)}) %collective-permute-start.4) | collective-permute-done | bytes 163872 | tf_op jit(solution)/shard_map/ppermute | solution.py:172
  37.3 1.0 %collective-permute-start.5 = (bf16[320,256]{1,0:T(8,128)(2,1)S(1)}, bf16[320,256]{1,0:T(8,128)(2,1)S(1)}, u32[]{:S(2)}, u32[]{:S(2)}) collective-permute-start(bf16[320,256]{1,0:T(8,128)(2,1)S(1)} %add_convert_fusion.1), channel_id=1, source_target_pairs={{0,8},{1,3},{2,10},{3,1},{4,12},{5,7},{6,14},{7,5},{8,0},{9,11},{1... | collective-permute-start | bytes 491528 | tf_op jit(solution)/shard_map/ppermute | solution.py:172
  38.3 4.0 %all-to-all-start.1 = ((bf16[8,32,256]{2,1,0:T(8,128)(2,1)}), bf16[8,32,256]{2,1,0:T(8,128)(2,1)S(1)}, u32[]{:S(2)}, u32[]{:S(2)}) async-start(bf16[8,32,256]{2,1,0:T(8,128)(2,1)} %bitcast.8), calls=%async_computation.1 | async-start | bytes 262144 | tf_op jit(solution)/shard_map/all_to_all | solution.py:230
  42.2 2.4 %collective-permute-done.5 = bf16[320,256]{1,0:T(8,128)(2,1)S(1)} collective-permute-done((bf16[320,256]{1,0:T(8,128)(2,1)S(1)}, bf16[320,256]{1,0:T(8,128)(2,1)S(1)}, u32[]{:S(2)}, u32[]{:S(2)}) %collective-permute-start.5) | collective-permute-done | bytes 163872 | tf_op jit(solution)/shard_map/ppermute | solution.py:172
  44.7 0.0 copy-start.4
  44.7 1.1 %collective-permute-start.6 = (bf16[320,256]{1,0:T(8,128)(2,1)S(1)}, bf16[320,256]{1,0:T(8,128)(2,1)S(1)}, u32[]{:S(2)}, u32[]{:S(2)}) collective-permute-start(bf16[320,256]{1,0:T(8,128)(2,1)S(1)} %add_convert_fusion.mine_ref), channel_id=1, source_target_pairs={{0,2},{1,5},{2,0},{3,7},{4,6},{5,1},{6,4},{7,3},{8,10},{9,13},{10,... | collective-permute-start | bytes 491528 | tf_op jit(solution)/shard_map/ppermute | solution.py:172
  45.8 1.2 %copy-done.10 = bf16[2048,256]{1,0:T(8,128)(2,1)S(1)} copy-done((bf16[2048,256]{1,0:T(8,128)(2,1)S(1)}, bf16[2048,256]{1,0:T(8,128)(2,1)}, u32[]{:S(2)}) %copy-start.10) | copy-done | bytes 1048600
  47.1 1.2 %home.1.home_ref = f32[1024,256]{1,0:T(8,128)S(1)} custom-call(s32[16,128]{1,0:T(8,128)S(1)} %bitcast.16, bf16[2048,256]{1,0:T(8,128)(2,1)S(1)} %copy-done.10), custom_call_target="tpu_custom_call" | custom-call | flops 1073741824 | bytes 2105344 | tf_op jit(solution)/shard_map/home/pallas_call | solution.py:145
  48.3 1.9 %all-to-all-done.1 = bf16[8,32,256]{2,1,0:T(8,128)(2,1)S(1)} async-done(((bf16[8,32,256]{2,1,0:T(8,128)(2,1)}), bf16[8,32,256]{2,1,0:T(8,128)(2,1)S(1)}, u32[]{:S(2)}, u32[]{:S(2)}) %all-to-all-start.1) | async-done | bytes 131104 | tf_op jit(solution)/shard_map/all_to_all | solution.py:230
  50.2 0.0 collective-permute-done.6.theirs_ref
  50.3 1.8 %finish.1 = (bf16[1024,256]{1,0:T(8,128)(2,1)}, f32[256,512]{1,0:T(8,128)}, f32[64,256]{1,0:T(8,128)}) custom-call(s32[2]{0:T(128)S(1)} %pad_add_fusion.where_ref, s32[2,128]{1,0:T(2,128)S(1)} %bitcast.18, bf16[256,256]{1,0:T(8,128)(2,1)S(1)} %bitcast.11, f32[1024,256]{1,0:T(8,128)S(1)} %home.1.home_ref, bf16[320,256]{1,0:T(8,128)(2,1)S(1)} %add_convert_fusion.mine_ref, ...), custom_call_target="tpu_custom_call" | custom-call | flops 134217728 | bytes 2622472 | tf_op jit(solution)/shard_map/finish/pallas_call | solution.py:145
  (25 shorter events, 0.2 us)
Async XLA Ops:
  0.6 16.8 %copy-start.3 = (s32[2048]{0:T(1024)S(1)}, s32[2048]{0:T(1024)}, u32[]{:S(2)}) copy-start(s32[2048]{0:T(1024)} %param.14) | copy-start | bytes 24580
  0.6 16.7 %copy-start.7 = (bf16[64,256]{1,0:T(8,128)(2,1)S(1)}, bf16[64,256]{1,0:T(8,128)(2,1)}, u32[]{:S(2)}) copy-start(bf16[64,256]{1,0:T(8,128)(2,1)} %wb_ref.3) | copy-start | bytes 98308
  0.7 16.7 %copy-start.5 = (bf16[64,2048]{1,0:T(8,128)(2,1)S(1)}, bf16[64,2048]{1,0:T(8,128)(2,1)}, u32[]{:S(2)}) copy-start(bf16[64,2048]{1,0:T(8,128)(2,1)} %basis_ref.3) | copy-start | bytes 786436
  0.7 16.7 %copy-start.8 = (s32[2048]{0:T(1024)S(1)}, s32[2048]{0:T(1024)}, u32[]{:S(2)}) copy-start(s32[2048]{0:T(1024)} %param.15) | copy-start | bytes 24580
  2.8 14.6 %all-to-all-start = ((bf16[8,32,256]{2,1,0:T(8,128)(2,1)}), bf16[8,32,256]{2,1,0:T(8,128)(2,1)S(1)}, u32[]{:S(2)}, u32[]{:S(2)}) async-start(bf16[8,32,256]{2,1,0:T(8,128)(2,1)} %bitcast.6), calls=%async_computation | async-start | bytes 262144 | tf_op jit(solution)/shard_map/all_to_all | solution.py:194
  10.0 13.7 %collective-permute-start.2 = (bf16[1024,256]{1,0:T(8,128)(2,1)}, bf16[1024,256]{1,0:T(8,128)(2,1)S(1)}, u32[]{:S(2)}, u32[]{:S(2)}) collective-permute-start(bf16[1024,256]{1,0:T(8,128)(2,1)} %cot_own_ref.1), channel_id=1, source_target_pairs={{0,1},{1,0},{2,3},{3,2},{4,5},{5,4},{6,7},{7,6},{8,9},{9,8},{10,11... | collective-permute-start | bytes 1572872 | tf_op jit(solution)/shard_map/ppermute | solution.py:195
  10.1 1.0 %copy-start = (bf16[1024,256]{1,0:T(8,128)(2,1)S(1)}, bf16[1024,256]{1,0:T(8,128)(2,1)}, u32[]{:S(2)}) copy-start(bf16[1024,256]{1,0:T(8,128)(2,1)} %edges_ref.1) | copy-start | bytes 1572868
  11.1 0.7 %copy-start.2 = (s32[2048]{0:T(1024)S(1)}, s32[2048]{0:T(1024)}, u32[]{:S(2)}) copy-start(s32[2048]{0:T(1024)} %param.14) | copy-start | bytes 24580
  17.4 4.0 %copy-start.6 = (bf16[256,512]{1,0:T(8,128)(2,1)S(1)}, bf16[256,512]{1,0:T(8,128)(2,1)}, u32[]{:S(2)}) copy-start(bf16[256,512]{1,0:T(8,128)(2,1)} %w_ref.3) | copy-start | bytes 786436
  17.4 6.3 %copy-start.1 = (bf16[1024,256]{1,0:T(8,128)(2,1)S(1)}, bf16[1024,256]{1,0:T(8,128)(2,1)}, u32[]{:S(2)}) copy-start(bf16[1024,256]{1,0:T(8,128)(2,1)} %cot_own_ref.1) | copy-start | bytes 1572868
  20.4 1.0 %copy-start.11 = (bf16[2048,256]{1,0:T(8,128)(2,1)}, bf16[2048,256]{1,0:T(8,128)(2,1)S(1)}, u32[]{:S(2)}) copy-start(bf16[2048,256]{1,0:T(8,128)(2,1)S(1)} %get-tuple-element.17.rows_ref) | copy-start | bytes 3145732
  21.4 2.3 %collective-permute-start = (bf16[1024,256]{1,0:T(8,128)(2,1)S(1)}, bf16[1024,256]{1,0:T(8,128)(2,1)S(1)}, u32[]{:S(2)}, u32[]{:S(2)}) collective-permute-start(bf16[1024,256]{1,0:T(8,128)(2,1)S(1)} %get-tuple-element.13.own_ref), channel_id=1, source_target_pairs={{0,1},{1,0},{2,3},{3,2},{4,5},{5,4},{6,7},{7,6},{8,9},{9,8},{10,11... | collective-permute-start | bytes 1572872 | tf_op jit(solution)/shard_map/ppermute | solution.py:205
  21.5 2.3 %collective-permute-start.1 = (bf16[256,512]{1,0:T(8,128)(2,1)S(1)}, bf16[256,512]{1,0:T(8,128)(2,1)S(1)}, u32[]{:S(2)}, u32[]{:S(2)}) collective-permute-start(bf16[256,512]{1,0:T(8,128)(2,1)S(1)} %copy-done.6), channel_id=1, source_target_pairs={{0,1},{1,0},{2,3},{3,2},{4,5},{5,4},{6,7},{7,6},{8,9},{9,8},{10,11... | collective-permute-start | bytes 786440 | tf_op jit(solution)/shard_map/ppermute | solution.py:195
  23.7 2.3 %copy-start.12 = (bf16[2048,256]{1,0:T(8,128)(2,1)S(1)}, bf16[2048,256]{1,0:T(8,128)(2,1)}, u32[]{:S(2)}) copy-start(bf16[2048,256]{1,0:T(8,128)(2,1)} %copy-done.11) | copy-start | bytes 3145732
  25.8 5.0 %collective-permute-start.3 = (bf16[256,256]{1,0:T(8,128)(2,1)S(1)}, bf16[256,256]{1,0:T(8,128)(2,1)S(1)}, u32[]{:S(2)}, u32[]{:S(2)}) collective-permute-start(bf16[256,256]{1,0:T(8,128)(2,1)S(1)} %get-tuple-element.21), channel_id=1, source_target_pairs={{0,2},{1,5},{2,0},{3,7},{4,6},{5,1},{6,4},{7,3},{8,10},{9,13},{10,... | collective-permute-start | bytes 393224 | tf_op jit(solution)/shard_map/ppermute | solution.py:172
  30.0 8.3 %copy-start.9 = (bf16[2048,256]{1,0:T(8,128)(2,1)}, bf16[2048,256]{1,0:T(8,128)(2,1)S(1)}, u32[]{:S(2)}) copy-start(bf16[2048,256]{1,0:T(8,128)(2,1)S(1)} %get-tuple-element.19.flow_ref) | copy-start | bytes 3145732
  30.9 6.4 %collective-permute-start.4 = (bf16[320,256]{1,0:T(8,128)(2,1)S(1)}, bf16[320,256]{1,0:T(8,128)(2,1)S(1)}, u32[]{:S(2)}, u32[]{:S(2)}) collective-permute-start(bf16[320,256]{1,0:T(8,128)(2,1)S(1)} %pad_maximum_fusion), channel_id=1, source_target_pairs={{0,4},{1,9},{2,6},{3,11},{4,0},{5,13},{6,2},{7,15},{8,12},{9,1},{1... | collective-permute-start | bytes 491528 | tf_op jit(solution)/shard_map/ppermute | solution.py:172
  37.3 7.3 %collective-permute-start.5 = (bf16[320,256]{1,0:T(8,128)(2,1)S(1)}, bf16[320,256]{1,0:T(8,128)(2,1)S(1)}, u32[]{:S(2)}, u32[]{:S(2)}) collective-permute-start(bf16[320,256]{1,0:T(8,128)(2,1)S(1)} %add_convert_fusion.1), channel_id=1, source_target_pairs={{0,8},{1,3},{2,10},{3,1},{4,12},{5,7},{6,14},{7,5},{8,0},{9,11},{1... | collective-permute-start | bytes 491528 | tf_op jit(solution)/shard_map/ppermute | solution.py:172
  38.3 12.0 %all-to-all-start.1 = ((bf16[8,32,256]{2,1,0:T(8,128)(2,1)}), bf16[8,32,256]{2,1,0:T(8,128)(2,1)S(1)}, u32[]{:S(2)}, u32[]{:S(2)}) async-start(bf16[8,32,256]{2,1,0:T(8,128)(2,1)} %bitcast.8), calls=%async_computation.1 | async-start | bytes 262144 | tf_op jit(solution)/shard_map/all_to_all | solution.py:230
  44.7 5.6 %copy-start.4 = (s32[1,256]{1,0:T(1,128)S(1)}, s32[1,256]{1,0:T(1,128)}, u32[]{:S(2)}) copy-start(s32[1,256]{1,0:T(1,128)} %param.13) | copy-start | bytes 3076
  44.7 5.6 %collective-permute-start.6 = (bf16[320,256]{1,0:T(8,128)(2,1)S(1)}, bf16[320,256]{1,0:T(8,128)(2,1)S(1)}, u32[]{:S(2)}, u32[]{:S(2)}) collective-permute-start(bf16[320,256]{1,0:T(8,128)(2,1)S(1)} %add_convert_fusion.mine_ref), channel_id=1, source_target_pairs={{0,2},{1,5},{2,0},{3,7},{4,6},{5,1},{6,4},{7,3},{8,10},{9,13},{10,... | collective-permute-start | bytes 491528 | tf_op jit(solution)/shard_map/ppermute | solution.py:172
  45.8 1.2 %copy-start.10 = (bf16[2048,256]{1,0:T(8,128)(2,1)S(1)}, bf16[2048,256]{1,0:T(8,128)(2,1)}, u32[]{:S(2)}) copy-start(bf16[2048,256]{1,0:T(8,128)(2,1)} %copy-done.9) | copy-start | bytes 3145732

commit v3 on v2

--- a/solution.py
+++ b/solution.py
@@ -52,10 +52,19 @@
     return dot((send_index[:, None] == rows[None, :]).astype(BF16), edges).astype(BF16)
 
 
-def near_kernel(slot_ref, edges_ref, out_ref):
+def near_kernel(where_ref, slot_ref, edges_ref, cot_own_hbm, cot_other_hbm, out_ref, cot_ref, sems):
+    width = edges_ref.shape[1]
+    side = where_ref[0]
+    copies = []
+    for k, (spot, hbm) in enumerate(((side, cot_own_hbm), (1 - side, cot_other_hbm))):
+        columns = pl.ds(pl.multiple_of(spot * width, width), width)
+        copies.append(pltpu.make_async_copy(hbm, cot_ref.at[:, columns], sems.at[k]))
+        copies[-1].start()
     for at in range(0, out_ref.shape[0], BLOCK):
         select = select_rows(slot_ref, at, BLOCK, edges_ref.shape[0], 0)
         out_ref[at : at + BLOCK, :] = dot(select, edges_ref[...]).astype(BF16)
+    for copy in copies:
+        copy.wait()
 
 
 def agg_kernel(slot_ref, out_index_ref, recv_ref, near_ref, basis_ref, wb_ref, rows_ref, agg_ref, msg_ref):
@@ -81,16 +90,14 @@
     turned_ref[...] = own_ref[...].T
 
 
-def slope_kernel(where_ref, pre_ref, turned_ref, other_ref, w_ref, cot_own_ref, cot_other_ref, keep_ref, send_ref, g_ref):
+def slope_kernel(where_ref, pre_ref, turned_ref, other_ref, w_ref, cot_ref, keep_ref, send_ref, g_ref):
     half = other_ref.shape[1]
     quarter = half // 2
-    side = where_ref[0]
     bit = where_ref[1]
-    for spot, cot_ref in ((side, cot_own_ref), (1 - side, cot_other_ref)):
-        columns = pl.ds(pl.multiple_of(spot * half, half), half)
+    for columns in (slice(0, half), slice(half, 2 * half)):
         pre = pre_ref[:, columns] + dot(other_ref[...], w_ref[:, columns])
         sig = 0.5 * jnp.tanh(0.5 * pre) + 0.5
-        g = cot_ref[...].astype(F32) * sig * (1.0 + pre * (1.0 - sig))
+        g = cot_ref[:, columns].astype(F32) * sig * (1.0 + pre * (1.0 - sig))
         g_ref[:, columns] = g.astype(BF16)
     for spot, ref in ((1 - bit, send_ref), (bit, keep_ref)):
         part = dot(turned_ref[pl.ds(pl.multiple_of(spot * quarter, quarter), quarter), :], g_ref[...]).astype(ref.dtype)
@@ -138,14 +145,16 @@
     edges_ref[...] = (home_ref[...] + dot(select, returned_ref[...])).astype(BF16)
 
 
-def call(kernel, outs, flops, *operands, scalars=0, scratch=(), name=None):
+def call(kernel, outs, flops, *operands, scalars=0, far=0, scratch=(), name=None):
     whole = pl.BlockSpec(memory_space=pltpu.VMEM)
     scalar = pl.BlockSpec(memory_space=pltpu.SMEM)
+    place = pl.BlockSpec(memory_space=pl.ANY)
+    near = len(operands) - far
     moved = sum(x.size * x.dtype.itemsize for x in operands) + sum(x.size * x.dtype.itemsize for x in outs)
     return pl.pallas_call(
         kernel,
         out_shape=outs,
-        in_specs=[scalar if i < scalars else whole for i in range(len(operands))],
+        in_specs=[scalar if i < scalars else whole if i < near else place for i in range(len(operands))],
         out_specs=[whole] * len(outs),
         scratch_shapes=scratch,
         compiler_params=pltpu.CompilerParams(vmem_limit_bytes=VMEM_LIMIT),
@@ -193,7 +202,16 @@
 
     received = lax.all_to_all(pack(send_index[0], edges), "graph", 0, 0, tiled=True)
     w_other, cot_other = lax.ppermute((w_up, out_grad), "mp", [(0, 1), (1, 0)])
-    (near,) = call(near_kernel, [shape(trips, half, BF16)], 0, slots, edges, name="near")
+    near, cot = call(
+        near_kernel,
+        [shape(trips, half, BF16), shape(edge_rows, 2 * half, BF16)],
+        0,
+        place, slots, edges, out_grad, cot_other,
+        scalars=1,
+        far=2,
+        scratch=[pltpu.SemaphoreType.DMA((2,))],
+        name="near",
+    )
     rows, agg = call(
         agg_kernel,
         [shape(trips, half, BF16), shape(edge_rows, half, BF16)],
@@ -214,7 +232,7 @@
         slope_kernel,
         [shape(half, half, F32), shape(half, half, BF16), shape(edge_rows, 2 * half, BF16)],
         8 * edge_rows * half * half,
-        place, pre_own, turned, agg_other, w_other, out_grad, cot_other,
+        place, pre_own, turned, agg_other, w_other, cot,
         scalars=1,
         name="slope",
     )

time: 52.5 us -> 52.2 us (level)
  local copies, waits for them, and re-layouts: 4.01 us -> 2.81 us
  Pallas kernels: 13.7 us -> 14.3 us
  starting transfers between devices: 14.4 us -> 15 us
    all_to_all x1, waiting for transfers between devices: 4.29 us -> 2.82 us  [on_device(): lax.all_to_all(pack(send_index[0], edges), 'graph', 0, 0, tiled=True)]
    unnamed x26 -> x18, local copies, waits for them, and re-layouts: 4.01 us -> 2.81 us
    ppermute x4, starting transfers between devices: 2.67 us -> 3.33 us  [swap(): return lax.ppermute(values, ('graph', 'mp'), pairs)]
    ppermute x4, waiting for transfers between devices: 9.35 us -> 9.98 us  [swap(): return lax.ppermute(values, ('graph', 'mp'), pairs)]
    pallas_call x7, Pallas kernels: 13.7 us -> 14.3 us  [call(): pl.pallas_call(kernel, out_shape=outs, in_specs=[scalar if i < scalars el...]
    all_to_all x1, waiting for transfers between devices: 1.94 us -> 2.48 us  [on_device(): returned = lax.all_to_all(leaving, 'graph', 0, 0, tiled=True)]
  transfers between devices with their start and end apart: 9 -> 9, of which waited for: 6 -> 7; matrix products, arithmetic and copies ran while one was open for 0% -> 4% of each run, Pallas kernels for 19% -> 14%
where the time goes in v3:
time: 52.2 us; the launch traced here: 51.8 us
  waiting for transfers between devices  16.6 us (32%)
  starting transfers between devices  15 us (29%)
  Pallas kernels  14.3 us (27%)
  local copies, waits for them, and re-layouts  2.81 us (5%)
  matrix products  2.07 us (4%)
  between operations  0.77 us (1%)
    pallas_call x7, Pallas kernels, call(): pl.pallas_call(kernel, out_shape=outs, in_specs=[scalar if i < scalars el...  14.3 us
    ppermute x4, waiting for transfers between devices, swap(): return lax.ppermute(values, ('graph', 'mp'), pairs)  9.98 us
    all_to_all x1, starting transfers between devices, on_device(): lax.all_to_all(pack(send_index[0], edges), 'graph', 0, 0, tiled=True)  6.82 us
    all_to_all x1, starting transfers between devices, on_device(): returned = lax.all_to_all(leaving, 'graph', 0, 0, tiled=True)  3.8 us
    ppermute x4, starting transfers between devices, swap(): return lax.ppermute(values, ('graph', 'mp'), pairs)  3.33 us
    all_to_all x1, waiting for transfers between devices, on_device(): lax.all_to_all(pack(send_index[0], edges), 'graph', 0, 0, tiled=True)  2.82 us
    unnamed x18, local copies, waits for them, and re-layouts  2.81 us
    all_to_all x1, waiting for transfers between devices, on_device(): returned = lax.all_to_all(leaving, 'graph', 0, 0, tiled=True)  2.48 us
  transfers between devices with their start and end apart: 9, of which 7 were waited for; matrix products, arithmetic and copies ran while one was open for 4% of the time, Pallas kernels for 14%

profile of v3, /device:TPU:0, one launch (start us, length us, event | category | flops | bytes accessed | tf_op | source)
XLA Modules:
  0.0 51.8 jit_solution(953498353767682470)
XLA Ops:
  0.6 0.0 copy-start.3
  0.7 0.5 %collective-permute-start = (bf16[1024,256]{1,0:T(8,128)(2,1)}, bf16[1024,256]{1,0:T(8,128)(2,1)S(1)}, u32[]{:S(2)}, u32[]{:S(2)}) collective-permute-start(bf16[1024,256]{1,0:T(8,128)(2,1)} %cot_own_hbm.1), channel_id=1, source_target_pairs={{0,1},{1,0},{2,3},{3,2},{4,5},{5,4},{6,7},{7,6},{8,9},{9,8},{10,11... | collective-permute-start | bytes 1572872 | tf_op jit(solution)/shard_map/ppermute | solution.py:204
  1.2 2.1 %convolution_convert_fusion = bf16[256,256]{1,0:T(8,128)(2,1)} fusion(bf16[1024,256]{1,0:T(8,128)(2,1)} %edges_ref.1, s32[256]{0:T(256)} %bitcast.17), kind=kOutput, calls=%fused_computation | convolution fusion | flops 134545408 | bytes 656384 | tf_op jit(solution)/shard_map/dot_general | solution.py:39
  3.3 6.8 %all-to-all-start = ((bf16[8,32,256]{2,1,0:T(8,128)(2,1)}), bf16[8,32,256]{2,1,0:T(8,128)(2,1)S(1)}, u32[]{:S(2)}, u32[]{:S(2)}) async-start(bf16[8,32,256]{2,1,0:T(8,128)(2,1)} %bitcast.6), calls=%async_computation | async-start | bytes 262144 | tf_op jit(solution)/shard_map/all_to_all | solution.py:203
  10.1 0.1 pad_add_fusion.where_ref
  10.2 0.0 collective-permute-done.cot_other_hbm
  10.2 1.0 %copy-done = bf16[1024,256]{1,0:T(8,128)(2,1)S(1)} copy-done((bf16[1024,256]{1,0:T(8,128)(2,1)S(1)}, bf16[1024,256]{1,0:T(8,128)(2,1)}, u32[]{:S(2)}) %copy-start) | copy-done | bytes 524312
  11.2 1.0 %copy-done.1 = bf16[1024,256]{1,0:T(8,128)(2,1)S(1)} copy-done((bf16[1024,256]{1,0:T(8,128)(2,1)S(1)}, bf16[1024,256]{1,0:T(8,128)(2,1)}, u32[]{:S(2)}) %copy-start.1) | copy-done | bytes 524312
  12.2 0.7 %copy-done.2 = s32[2048]{0:T(1024)S(1)} copy-done((s32[2048]{0:T(1024)S(1)}, s32[2048]{0:T(1024)}, u32[]{:S(2)}) %copy-start.2) | copy-done | bytes 8216
  12.9 1.9 %near.1 = (bf16[2048,256]{1,0:T(8,128)(2,1)S(1)}, bf16[1024,512]{1,0:T(8,128)(2,1)S(1)}) custom-call(s32[2]{0:T(128)S(1)} %pad_add_fusion.where_ref, s32[16,128]{1,0:T(8,128)S(1)} %bitcast.13, bf16[1024,256]{1,0:T(8,128)(2,1)S(1)} %copy-done, bf16[1024,256]{1,0:T(8,128)(2,1)S(1)} %copy-done.1, bf16[1024,256]{1,0:T(8,128)(2,1)S(1)} %collective-permute-done.cot_other_hbm), custom_call_target="tpu_custom_call" | custom-call | bytes 3678216 | tf_op jit(solution)/shard_map/near/pallas_call | solution.py:154
  14.9 2.8 %all-to-all-done = bf16[8,32,256]{2,1,0:T(8,128)(2,1)S(1)} async-done(((bf16[8,32,256]{2,1,0:T(8,128)(2,1)}), bf16[8,32,256]{2,1,0:T(8,128)(2,1)S(1)}, u32[]{:S(2)}, u32[]{:S(2)}) %all-to-all-start) | async-done | bytes 131104 | tf_op jit(solution)/shard_map/all_to_all | solution.py:203
  17.7 0.0 copy-start.6
  17.7 3.0 %agg.1 = (bf16[2048,256]{1,0:T(8,128)(2,1)S(1)}, bf16[1024,256]{1,0:T(8,128)(2,1)S(1)}) custom-call(s32[16,128]{1,0:T(8,128)S(1)} %bitcast.14, s32[16,128]{1,0:T(8,128)S(1)} %bitcast.19, bf16[256,256]{1,0:T(8,128)(2,1)S(1)} %bitcast.12, bf16[2048,256]{1,0:T(8,128)(2,1)S(1)} %get-tuple-element.15.near_ref, bf16[64,2048]{1,0:T(8,128)(2,1)S(1)} %copy-done.5, ...), custom_call_target="tpu_custom_call" | custom-call | flops 2415919104 | bytes 3063808 | tf_op jit(solution)/shard_map/agg/pallas_call | solution.py:154
  20.8 0.1 collective-permute-start.1
  20.9 0.5 collective-permute-start.2
  21.3 0.4 ready.1
  21.8 1.3 %collective-permute-done.2.w_ref = bf16[256,512]{1,0:T(8,128)(2,1)S(1)} collective-permute-done((bf16[256,512]{1,0:T(8,128)(2,1)S(1)}, bf16[256,512]{1,0:T(8,128)(2,1)S(1)}, u32[]{:S(2)}, u32[]{:S(2)}) %collective-permute-start.2) | collective-permute-done | bytes 262176 | tf_op jit(solution)/shard_map/ppermute | solution.py:204
  23.1 1.9 %slope.1 = (f32[256,256]{1,0:T(8,128)S(1)}, bf16[256,256]{1,0:T(8,128)(2,1)S(1)}, bf16[1024,512]{1,0:T(8,128)(2,1)S(1)}) custom-call(s32[2]{0:T(128)S(1)} %pad_add_fusion.where_ref, f32[1024,512]{1,0:T(8,128)S(1)} %get-tuple-element.17.pre_ref, bf16[256,1024]{1,0:T(8,128)(2,1)S(1)} %get-tuple-element.18.turned_ref, ...), custom_call_target="tpu_custom_call" | custom-call | flops 536870912 | bytes 5898248 | tf_op jit(solution)/shard_map/slope/pallas_call | solution.py:154
  25.1 0.3 collective-permute-start.3
  25.4 3.9 %spread.1 = (bf16[2048,256]{1,0:T(8,128)(2,1)S(1)}, bf16[256,256]{1,0:T(8,128)(2,1)}, bf16[64,256]{1,0:T(8,128)(2,1)S(1)}) custom-call(s32[16,128]{1,0:T(8,128)S(1)} %bitcast.15, s32[16,128]{1,0:T(8,128)S(1)} %bitcast.20, bf16[1024,512]{1,0:T(8,128)(2,1)S(1)} %get-tuple-element.20.g_ref, bf16[256,512]{1,0:T(8,128)(2,1)S(1)} %copy-done.6, ...), custom_call_target="tpu_custom_call" | custom-call | flops 1342177280 | bytes 3883008 | tf_op jit(solution)/shard_map/spread/pallas_call | solution.py:154
  29.3 0.8 %collective-permute-done.3 = bf16[256,256]{1,0:T(8,128)(2,1)S(1)} collective-permute-done((bf16[256,256]{1,0:T(8,128)(2,1)S(1)}, bf16[256,256]{1,0:T(8,128)(2,1)S(1)}, u32[]{:S(2)}, u32[]{:S(2)}) %collective-permute-start.3) | collective-permute-done | bytes 131104 | tf_op jit(solution)/shard_map/ppermute | solution.py:181
  30.1 0.3 collective-permute-start.4
  30.4 6.1 %collective-permute-done.4 = bf16[320,256]{1,0:T(8,128)(2,1)S(1)} collective-permute-done((bf16[320,256]{1,0:T(8,128)(2,1)S(1)}, bf16[320,256]{1,0:T(8,128)(2,1)S(1)}, u32[]{:S(2)}, u32[]{:S(2)}) %collective-permute-start.4) | collective-permute-done | bytes 163872 | tf_op jit(solution)/shard_map/ppermute | solution.py:181
  36.5 1.1 %collective-permute-start.5 = (bf16[320,256]{1,0:T(8,128)(2,1)S(1)}, bf16[320,256]{1,0:T(8,128)(2,1)S(1)}, u32[]{:S(2)}, u32[]{:S(2)}) collective-permute-start(bf16[320,256]{1,0:T(8,128)(2,1)S(1)} %add_convert_fusion.1), channel_id=1, source_target_pairs={{0,8},{1,3},{2,10},{3,1},{4,12},{5,7},{6,14},{7,5},{8,0},{9,11},{1... | collective-permute-start | bytes 491528 | tf_op jit(solution)/shard_map/ppermute | solution.py:181
  37.7 3.8 %all-to-all-start.1 = ((bf16[8,32,256]{2,1,0:T(8,128)(2,1)}), bf16[8,32,256]{2,1,0:T(8,128)(2,1)S(1)}, u32[]{:S(2)}, u32[]{:S(2)}) async-start(bf16[8,32,256]{2,1,0:T(8,128)(2,1)} %bitcast.8), calls=%async_computation.1 | async-start | bytes 262144 | tf_op jit(solution)/shard_map/all_to_all | solution.py:248
  41.5 2.8 %collective-permute-done.5 = bf16[320,256]{1,0:T(8,128)(2,1)S(1)} collective-permute-done((bf16[320,256]{1,0:T(8,128)(2,1)S(1)}, bf16[320,256]{1,0:T(8,128)(2,1)S(1)}, u32[]{:S(2)}, u32[]{:S(2)}) %collective-permute-start.5) | collective-permute-done | bytes 163872 | tf_op jit(solution)/shard_map/ppermute | solution.py:181
  44.4 0.0 copy-start.4
  44.4 1.6 %collective-permute-start.6 = (bf16[320,256]{1,0:T(8,128)(2,1)S(1)}, bf16[320,256]{1,0:T(8,128)(2,1)S(1)}, u32[]{:S(2)}, u32[]{:S(2)}) collective-permute-start(bf16[320,256]{1,0:T(8,128)(2,1)S(1)} %add_convert_fusion.mine_ref), channel_id=1, source_target_pairs={{0,2},{1,5},{2,0},{3,7},{4,6},{5,1},{6,4},{7,3},{8,10},{9,13},{10,... | collective-permute-start | bytes 491528 | tf_op jit(solution)/shard_map/ppermute | solution.py:181
  46.0 1.2 %home.1.home_ref = f32[1024,256]{1,0:T(8,128)S(1)} custom-call(s32[16,128]{1,0:T(8,128)S(1)} %bitcast.16, bf16[2048,256]{1,0:T(8,128)(2,1)S(1)} %get-tuple-element.23.flow_ref), custom_call_target="tpu_custom_call" | custom-call | flops 1073741824 | bytes 2105344 | tf_op jit(solution)/shard_map/home/pallas_call | solution.py:154
  47.2 2.5 %all-to-all-done.1 = bf16[8,32,256]{2,1,0:T(8,128)(2,1)S(1)} async-done(((bf16[8,32,256]{2,1,0:T(8,128)(2,1)}), bf16[8,32,256]{2,1,0:T(8,128)(2,1)S(1)}, u32[]{:S(2)}, u32[]{:S(2)}) %all-to-all-start.1) | async-done | bytes 131104 | tf_op jit(solution)/shard_map/all_to_all | solution.py:248
  49.7 0.3 collective-permute-done.6.theirs_ref
  49.9 1.8 %finish.1 = (bf16[1024,256]{1,0:T(8,128)(2,1)}, f32[256,512]{1,0:T(8,128)}, f32[64,256]{1,0:T(8,128)}) custom-call(s32[2]{0:T(128)S(1)} %pad_add_fusion.where_ref, s32[2,128]{1,0:T(2,128)S(1)} %bitcast.18, bf16[256,256]{1,0:T(8,128)(2,1)S(1)} %bitcast.11, f32[1024,256]{1,0:T(8,128)S(1)} %home.1.home_ref, bf16[320,256]{1,0:T(8,128)(2,1)S(1)} %add_convert_fusion.mine_ref, ...), custom_call_target="tpu_custom_call" | custom-call | flops 134217728 | bytes 2622472 | tf_op jit(solution)/shard_map/finish/pallas_call | solution.py:154
  (17 shorter events, 0.1 us)
Async XLA Ops:
  0.6 17.1 %copy-start.3 = (s32[2048]{0:T(1024)S(1)}, s32[2048]{0:T(1024)}, u32[]{:S(2)}) copy-start(s32[2048]{0:T(1024)} %param.14) | copy-start | bytes 24580
  0.6 17.1 %copy-start.7 = (bf16[64,256]{1,0:T(8,128)(2,1)S(1)}, bf16[64,256]{1,0:T(8,128)(2,1)}, u32[]{:S(2)}) copy-start(bf16[64,256]{1,0:T(8,128)(2,1)} %wb_ref.3) | copy-start | bytes 98308
  0.7 17.1 %copy-start.5 = (bf16[64,2048]{1,0:T(8,128)(2,1)S(1)}, bf16[64,2048]{1,0:T(8,128)(2,1)}, u32[]{:S(2)}) copy-start(bf16[64,2048]{1,0:T(8,128)(2,1)} %basis_ref.3) | copy-start | bytes 786436
  0.7 17.1 %copy-start.8 = (s32[2048]{0:T(1024)S(1)}, s32[2048]{0:T(1024)}, u32[]{:S(2)}) copy-start(s32[2048]{0:T(1024)} %param.15) | copy-start | bytes 24580
  0.7 9.5 %collective-permute-start = (bf16[1024,256]{1,0:T(8,128)(2,1)}, bf16[1024,256]{1,0:T(8,128)(2,1)S(1)}, u32[]{:S(2)}, u32[]{:S(2)}) collective-permute-start(bf16[1024,256]{1,0:T(8,128)(2,1)} %cot_own_hbm.1), channel_id=1, source_target_pairs={{0,1},{1,0},{2,3},{3,2},{4,5},{5,4},{6,7},{7,6},{8,9},{9,8},{10,11... | collective-permute-start | bytes 1572872 | tf_op jit(solution)/shard_map/ppermute | solution.py:204
  3.3 14.5 %all-to-all-start = ((bf16[8,32,256]{2,1,0:T(8,128)(2,1)}), bf16[8,32,256]{2,1,0:T(8,128)(2,1)S(1)}, u32[]{:S(2)}, u32[]{:S(2)}) async-start(bf16[8,32,256]{2,1,0:T(8,128)(2,1)} %bitcast.6), calls=%async_computation | async-start | bytes 262144 | tf_op jit(solution)/shard_map/all_to_all | solution.py:203
  10.2 1.0 %copy-start = (bf16[1024,256]{1,0:T(8,128)(2,1)S(1)}, bf16[1024,256]{1,0:T(8,128)(2,1)}, u32[]{:S(2)}) copy-start(bf16[1024,256]{1,0:T(8,128)(2,1)} %edges_ref.1) | copy-start | bytes 1572868
  11.2 1.0 %copy-start.1 = (bf16[1024,256]{1,0:T(8,128)(2,1)S(1)}, bf16[1024,256]{1,0:T(8,128)(2,1)}, u32[]{:S(2)}) copy-start(bf16[1024,256]{1,0:T(8,128)(2,1)} %cot_own_hbm.1) | copy-start | bytes 1572868
  12.2 0.7 %copy-start.2 = (s32[2048]{0:T(1024)S(1)}, s32[2048]{0:T(1024)}, u32[]{:S(2)}) copy-start(s32[2048]{0:T(1024)} %param.14) | copy-start | bytes 24580
  17.7 3.1 %copy-start.6 = (bf16[256,512]{1,0:T(8,128)(2,1)S(1)}, bf16[256,512]{1,0:T(8,128)(2,1)}, u32[]{:S(2)}) copy-start(bf16[256,512]{1,0:T(8,128)(2,1)} %w_ref.3) | copy-start | bytes 786436
  20.8 2.4 %collective-permute-start.1 = (bf16[1024,256]{1,0:T(8,128)(2,1)S(1)}, bf16[1024,256]{1,0:T(8,128)(2,1)S(1)}, u32[]{:S(2)}, u32[]{:S(2)}) collective-permute-start(bf16[1024,256]{1,0:T(8,128)(2,1)S(1)} %get-tuple-element.16.own_ref), channel_id=1, source_target_pairs={{0,1},{1,0},{2,3},{3,2},{4,5},{5,4},{6,7},{7,6},{8,9},{9,8},{10,11... | collective-permute-start | bytes 1572872 | tf_op jit(solution)/shard_map/ppermute | solution.py:223
  20.9 2.3 %collective-permute-start.2 = (bf16[256,512]{1,0:T(8,128)(2,1)S(1)}, bf16[256,512]{1,0:T(8,128)(2,1)S(1)}, u32[]{:S(2)}, u32[]{:S(2)}) collective-permute-start(bf16[256,512]{1,0:T(8,128)(2,1)S(1)} %copy-done.6), channel_id=1, source_target_pairs={{0,1},{1,0},{2,3},{3,2},{4,5},{5,4},{6,7},{7,6},{8,9},{9,8},{10,11... | collective-permute-start | bytes 786440 | tf_op jit(solution)/shard_map/ppermute | solution.py:204
  25.1 5.0 %collective-permute-start.3 = (bf16[256,256]{1,0:T(8,128)(2,1)S(1)}, bf16[256,256]{1,0:T(8,128)(2,1)S(1)}, u32[]{:S(2)}, u32[]{:S(2)}) collective-permute-start(bf16[256,256]{1,0:T(8,128)(2,1)S(1)} %get-tuple-element.25), channel_id=1, source_target_pairs={{0,2},{1,5},{2,0},{3,7},{4,6},{5,1},{6,4},{7,3},{8,10},{9,13},{10,... | collective-permute-start | bytes 393224 | tf_op jit(solution)/shard_map/ppermute | solution.py:181
  30.1 6.3 %collective-permute-start.4 = (bf16[320,256]{1,0:T(8,128)(2,1)S(1)}, bf16[320,256]{1,0:T(8,128)(2,1)S(1)}, u32[]{:S(2)}, u32[]{:S(2)}) collective-permute-start(bf16[320,256]{1,0:T(8,128)(2,1)S(1)} %pad_maximum_fusion), channel_id=1, source_target_pairs={{0,4},{1,9},{2,6},{3,11},{4,0},{5,13},{6,2},{7,15},{8,12},{9,1},{1... | collective-permute-start | bytes 491528 | tf_op jit(solution)/shard_map/ppermute | solution.py:181
  36.5 7.8 %collective-permute-start.5 = (bf16[320,256]{1,0:T(8,128)(2,1)S(1)}, bf16[320,256]{1,0:T(8,128)(2,1)S(1)}, u32[]{:S(2)}, u32[]{:S(2)}) collective-permute-start(bf16[320,256]{1,0:T(8,128)(2,1)S(1)} %add_convert_fusion.1), channel_id=1, source_target_pairs={{0,8},{1,3},{2,10},{3,1},{4,12},{5,7},{6,14},{7,5},{8,0},{9,11},{1... | collective-permute-start | bytes 491528 | tf_op jit(solution)/shard_map/ppermute | solution.py:181
  37.7 12.0 %all-to-all-start.1 = ((bf16[8,32,256]{2,1,0:T(8,128)(2,1)}), bf16[8,32,256]{2,1,0:T(8,128)(2,1)S(1)}, u32[]{:S(2)}, u32[]{:S(2)}) async-start(bf16[8,32,256]{2,1,0:T(8,128)(2,1)} %bitcast.8), calls=%async_computation.1 | async-start | bytes 262144 | tf_op jit(solution)/shard_map/all_to_all | solution.py:248
  44.4 5.6 %copy-start.4 = (s32[1,256]{1,0:T(1,128)S(1)}, s32[1,256]{1,0:T(1,128)}, u32[]{:S(2)}) copy-start(s32[1,256]{1,0:T(1,128)} %param.13) | copy-start | bytes 3076
  44.4 5.6 %collective-permute-start.6 = (bf16[320,256]{1,0:T(8,128)(2,1)S(1)}, bf16[320,256]{1,0:T(8,128)(2,1)S(1)}, u32[]{:S(2)}, u32[]{:S(2)}) collective-permute-start(bf16[320,256]{1,0:T(8,128)(2,1)S(1)} %add_convert_fusion.mine_ref), channel_id=1, source_target_pairs={{0,2},{1,5},{2,0},{3,7},{4,6},{5,1},{6,4},{7,3},{8,10},{9,13},{10,... | collective-permute-start | bytes 491528 | tf_op jit(solution)/shard_map/ppermute | solution.py:181

commit v4 on v3

--- a/solution.py
+++ b/solution.py
@@ -49,7 +49,7 @@
 
 def pack(send_index, edges):
     rows = jnp.arange(edges.shape[0], dtype=jnp.int32)
-    return dot((send_index[:, None] == rows[None, :]).astype(BF16), edges).astype(BF16)
+    return jnp.dot((send_index[:, None] == rows[None, :]).astype(BF16), edges, preferred_element_type=BF16)
 
 
 def near_kernel(where_ref, slot_ref, edges_ref, cot_own_hbm, cot_other_hbm, out_ref, cot_ref, sems):
@@ -200,8 +200,9 @@
     slots = trip_slot.reshape(trips // LANES, LANES)
     outs = trip_out.reshape(trips // LANES, LANES)
 
-    received = lax.all_to_all(pack(send_index[0], edges), "graph", 0, 0, tiled=True)
-    w_other, cot_other = lax.ppermute((w_up, out_grad), "mp", [(0, 1), (1, 0)])
+    packed, cot_mine = lax.optimization_barrier((pack(send_index[0], edges), out_grad))
+    received = lax.all_to_all(packed, "graph", 0, 0, tiled=True)
+    w_other, cot_other = lax.ppermute((w_up, cot_mine), "mp", [(0, 1), (1, 0)])
     near, cot = call(
         near_kernel,
         [shape(trips, half, BF16), shape(edge_rows, 2 * half, BF16)],

time: 52.2 us -> 52.2 us (level)
  transfers between devices with their start and end apart: 9 -> 9, of which waited for: 7 -> 7; matrix products, arithmetic and copies ran while one was open for 4% -> 0% of each run, Pallas kernels for 14% -> 15%
where the time goes in v4:
time: 52.2 us; the launch traced here: 51.7 us
  waiting for transfers between devices  16.6 us (32%)
  starting transfers between devices  14.9 us (29%)
  Pallas kernels  14.3 us (27%)
  local copies, waits for them, and re-layouts  2.81 us (5%)
  matrix products  2.11 us (4%)
  between operations  0.77 us (1%)
    pallas_call x7, Pallas kernels, call(): pl.pallas_call(kernel, out_shape=outs, in_specs=[scalar if i < scalars el...  14.3 us
    ppermute x4, waiting for transfers between devices, swap(): return lax.ppermute(values, ('graph', 'mp'), pairs)  9.98 us
    all_to_all x1, starting transfers between devices, on_device(): received = lax.all_to_all(packed, 'graph', 0, 0, tiled=True)  6.8 us
    all_to_all x1, starting transfers between devices, on_device(): returned = lax.all_to_all(leaving, 'graph', 0, 0, tiled=True)  3.8 us
    ppermute x4, starting transfers between devices, swap(): return lax.ppermute(values, ('graph', 'mp'), pairs)  3.32 us
    all_to_all x1, waiting for transfers between devices, on_device(): received = lax.all_to_all(packed, 'graph', 0, 0, tiled=True)  2.84 us
    unnamed x18, local copies, waits for them, and re-layouts  2.81 us
    all_to_all x1, waiting for transfers between devices, on_device(): returned = lax.all_to_all(leaving, 'graph', 0, 0, tiled=True)  2.47 us
  transfers between devices with their start and end apart: 9, of which 7 were waited for; matrix products, arithmetic and copies ran while one was open for 0% of the time, Pallas kernels for 15%

profile of v4, /device:TPU:0, one launch (start us, length us, event | category | flops | bytes accessed | tf_op | source)
XLA Modules:
  0.0 51.7 jit_solution(11054165782003970785)
XLA Ops:
  0.6 0.0 copy-start.3
  0.7 2.1 %fusion = bf16[256,256]{1,0:T(8,128)(2,1)} fusion(bf16[1024,256]{1,0:T(8,128)(2,1)} %edges_ref.1, s32[256]{0:T(256)} %bitcast.17), kind=kOutput, calls=%fused_computation.1 | convolution fusion | flops 134479872 | bytes 656384 | tf_op jit(solution)/shard_map/dot_general | solution.py:52
  2.8 0.5 collective-permute-start
  3.2 6.8 %all-to-all-start = ((bf16[8,32,256]{2,1,0:T(8,128)(2,1)}), bf16[8,32,256]{2,1,0:T(8,128)(2,1)S(1)}, u32[]{:S(2)}, u32[]{:S(2)}) async-start(bf16[8,32,256]{2,1,0:T(8,128)(2,1)} %bitcast.6), calls=%async_computation | async-start | bytes 262144 | tf_op jit(solution)/shard_map/all_to_all | solution.py:204
  10.0 0.1 pad_add_fusion.where_ref
  10.1 0.0 collective-permute-done.cot_other_hbm
  10.1 1.0 %copy-done = bf16[1024,256]{1,0:T(8,128)(2,1)S(1)} copy-done((bf16[1024,256]{1,0:T(8,128)(2,1)S(1)}, bf16[1024,256]{1,0:T(8,128)(2,1)}, u32[]{:S(2)}) %copy-start) | copy-done | bytes 524312
  11.2 1.0 %copy-done.1 = bf16[1024,256]{1,0:T(8,128)(2,1)S(1)} copy-done((bf16[1024,256]{1,0:T(8,128)(2,1)S(1)}, bf16[1024,256]{1,0:T(8,128)(2,1)}, u32[]{:S(2)}) %copy-start.1) | copy-done | bytes 524312
  12.2 0.7 %copy-done.2 = s32[2048]{0:T(1024)S(1)} copy-done((s32[2048]{0:T(1024)S(1)}, s32[2048]{0:T(1024)}, u32[]{:S(2)}) %copy-start.2) | copy-done | bytes 8216
  12.9 1.9 %near.1 = (bf16[2048,256]{1,0:T(8,128)(2,1)S(1)}, bf16[1024,512]{1,0:T(8,128)(2,1)S(1)}) custom-call(s32[2]{0:T(128)S(1)} %pad_add_fusion.where_ref, s32[16,128]{1,0:T(8,128)S(1)} %bitcast.13, bf16[1024,256]{1,0:T(8,128)(2,1)S(1)} %copy-done, bf16[1024,256]{1,0:T(8,128)(2,1)S(1)} %copy-done.1, bf16[1024,256]{1,0:T(8,128)(2,1)S(1)} %collective-permute-done.cot_other_hbm), custom_call_target="tpu_custom_call" | custom-call | bytes 3678216 | tf_op jit(solution)/shard_map/near/pallas_call | solution.py:154
  14.9 2.8 %all-to-all-done = bf16[8,32,256]{2,1,0:T(8,128)(2,1)S(1)} async-done(((bf16[8,32,256]{2,1,0:T(8,128)(2,1)}), bf16[8,32,256]{2,1,0:T(8,128)(2,1)S(1)}, u32[]{:S(2)}, u32[]{:S(2)}) %all-to-all-start) | async-done | bytes 131104 | tf_op jit(solution)/shard_map/all_to_all | solution.py:204
  17.7 0.0 copy-start.6
  17.7 3.0 %agg.1 = (bf16[2048,256]{1,0:T(8,128)(2,1)S(1)}, bf16[1024,256]{1,0:T(8,128)(2,1)S(1)}) custom-call(s32[16,128]{1,0:T(8,128)S(1)} %bitcast.14, s32[16,128]{1,0:T(8,128)S(1)} %bitcast.19, bf16[256,256]{1,0:T(8,128)(2,1)S(1)} %bitcast.12, bf16[2048,256]{1,0:T(8,128)(2,1)S(1)} %get-tuple-element.19.near_ref, bf16[64,2048]{1,0:T(8,128)(2,1)S(1)} %copy-done.5, ...), custom_call_target="tpu_custom_call" | custom-call | flops 2415919104 | bytes 3063808 | tf_op jit(solution)/shard_map/agg/pallas_call | solution.py:154
  20.7 0.1 collective-permute-start.1
  20.8 0.5 collective-permute-start.2
  21.3 0.4 ready.1
  21.8 1.3 %collective-permute-done.2.w_ref = bf16[256,512]{1,0:T(8,128)(2,1)S(1)} collective-permute-done((bf16[256,512]{1,0:T(8,128)(2,1)S(1)}, bf16[256,512]{1,0:T(8,128)(2,1)S(1)}, u32[]{:S(2)}, u32[]{:S(2)}) %collective-permute-start.2) | collective-permute-done | bytes 262176 | tf_op jit(solution)/shard_map/ppermute | solution.py:205
  23.1 1.9 %slope.1 = (f32[256,256]{1,0:T(8,128)S(1)}, bf16[256,256]{1,0:T(8,128)(2,1)S(1)}, bf16[1024,512]{1,0:T(8,128)(2,1)S(1)}) custom-call(s32[2]{0:T(128)S(1)} %pad_add_fusion.where_ref, f32[1024,512]{1,0:T(8,128)S(1)} %get-tuple-element.21.pre_ref, bf16[256,1024]{1,0:T(8,128)(2,1)S(1)} %get-tuple-element.22.turned_ref, ...), custom_call_target="tpu_custom_call" | custom-call | flops 536870912 | bytes 5898248 | tf_op jit(solution)/shard_map/slope/pallas_call | solution.py:154
  25.0 0.3 collective-permute-start.3
  25.3 3.9 %spread.1 = (bf16[2048,256]{1,0:T(8,128)(2,1)S(1)}, bf16[256,256]{1,0:T(8,128)(2,1)}, bf16[64,256]{1,0:T(8,128)(2,1)S(1)}) custom-call(s32[16,128]{1,0:T(8,128)S(1)} %bitcast.15, s32[16,128]{1,0:T(8,128)S(1)} %bitcast.20, bf16[1024,512]{1,0:T(8,128)(2,1)S(1)} %get-tuple-element.24.g_ref, bf16[256,512]{1,0:T(8,128)(2,1)S(1)} %copy-done.6, ...), custom_call_target="tpu_custom_call" | custom-call | flops 1342177280 | bytes 3883008 | tf_op jit(solution)/shard_map/spread/pallas_call | solution.py:154
  29.2 0.8 %collective-permute-done.3 = bf16[256,256]{1,0:T(8,128)(2,1)S(1)} collective-permute-done((bf16[256,256]{1,0:T(8,128)(2,1)S(1)}, bf16[256,256]{1,0:T(8,128)(2,1)S(1)}, u32[]{:S(2)}, u32[]{:S(2)}) %collective-permute-start.3) | collective-permute-done | bytes 131104 | tf_op jit(solution)/shard_map/ppermute | solution.py:181
  30.1 0.3 collective-permute-start.4
  30.4 6.1 %collective-permute-done.4 = bf16[320,256]{1,0:T(8,128)(2,1)S(1)} collective-permute-done((bf16[320,256]{1,0:T(8,128)(2,1)S(1)}, bf16[320,256]{1,0:T(8,128)(2,1)S(1)}, u32[]{:S(2)}, u32[]{:S(2)}) %collective-permute-start.4) | collective-permute-done | bytes 163872 | tf_op jit(solution)/shard_map/ppermute | solution.py:181
  36.5 1.1 %collective-permute-start.5 = (bf16[320,256]{1,0:T(8,128)(2,1)S(1)}, bf16[320,256]{1,0:T(8,128)(2,1)S(1)}, u32[]{:S(2)}, u32[]{:S(2)}) collective-permute-start(bf16[320,256]{1,0:T(8,128)(2,1)S(1)} %add_convert_fusion.1), channel_id=1, source_target_pairs={{0,8},{1,3},{2,10},{3,1},{4,12},{5,7},{6,14},{7,5},{8,0},{9,11},{1... | collective-permute-start | bytes 491528 | tf_op jit(solution)/shard_map/ppermute | solution.py:181
  37.6 3.8 %all-to-all-start.1 = ((bf16[8,32,256]{2,1,0:T(8,128)(2,1)}), bf16[8,32,256]{2,1,0:T(8,128)(2,1)S(1)}, u32[]{:S(2)}, u32[]{:S(2)}) async-start(bf16[8,32,256]{2,1,0:T(8,128)(2,1)} %bitcast.8), calls=%async_computation.1 | async-start | bytes 262144 | tf_op jit(solution)/shard_map/all_to_all | solution.py:249
  41.4 2.8 %collective-permute-done.5 = bf16[320,256]{1,0:T(8,128)(2,1)S(1)} collective-permute-done((bf16[320,256]{1,0:T(8,128)(2,1)S(1)}, bf16[320,256]{1,0:T(8,128)(2,1)S(1)}, u32[]{:S(2)}, u32[]{:S(2)}) %collective-permute-start.5) | collective-permute-done | bytes 163872 | tf_op jit(solution)/shard_map/ppermute | solution.py:181
  44.3 0.0 copy-start.4
  44.3 1.6 %collective-permute-start.6 = (bf16[320,256]{1,0:T(8,128)(2,1)S(1)}, bf16[320,256]{1,0:T(8,128)(2,1)S(1)}, u32[]{:S(2)}, u32[]{:S(2)}) collective-permute-start(bf16[320,256]{1,0:T(8,128)(2,1)S(1)} %add_convert_fusion.mine_ref), channel_id=1, source_target_pairs={{0,2},{1,5},{2,0},{3,7},{4,6},{5,1},{6,4},{7,3},{8,10},{9,13},{10,... | collective-permute-start | bytes 491528 | tf_op jit(solution)/shard_map/ppermute | solution.py:181
  45.9 1.2 %home.1.home_ref = f32[1024,256]{1,0:T(8,128)S(1)} custom-call(s32[16,128]{1,0:T(8,128)S(1)} %bitcast.16, bf16[2048,256]{1,0:T(8,128)(2,1)S(1)} %get-tuple-element.27.flow_ref), custom_call_target="tpu_custom_call" | custom-call | flops 1073741824 | bytes 2105344 | tf_op jit(solution)/shard_map/home/pallas_call | solution.py:154
  47.2 2.5 %all-to-all-done.1 = bf16[8,32,256]{2,1,0:T(8,128)(2,1)S(1)} async-done(((bf16[8,32,256]{2,1,0:T(8,128)(2,1)}), bf16[8,32,256]{2,1,0:T(8,128)(2,1)S(1)}, u32[]{:S(2)}, u32[]{:S(2)}) %all-to-all-start.1) | async-done | bytes 131104 | tf_op jit(solution)/shard_map/all_to_all | solution.py:249
  49.6 0.3 collective-permute-done.6.theirs_ref
  49.9 1.8 %finish.1 = (bf16[1024,256]{1,0:T(8,128)(2,1)}, f32[256,512]{1,0:T(8,128)}, f32[64,256]{1,0:T(8,128)}) custom-call(s32[2]{0:T(128)S(1)} %pad_add_fusion.where_ref, s32[2,128]{1,0:T(2,128)S(1)} %bitcast.18, bf16[256,256]{1,0:T(8,128)(2,1)S(1)} %bitcast.11, f32[1024,256]{1,0:T(8,128)S(1)} %home.1.home_ref, bf16[320,256]{1,0:T(8,128)(2,1)S(1)} %add_convert_fusion.mine_ref, ...), custom_call_target="tpu_custom_call" | custom-call | flops 134217728 | bytes 2622472 | tf_op jit(solution)/shard_map/finish/pallas_call | solution.py:154
  (17 shorter events, 0.2 us)
Async XLA Ops:
  0.6 17.1 %copy-start.3 = (s32[2048]{0:T(1024)S(1)}, s32[2048]{0:T(1024)}, u32[]{:S(2)}) copy-start(s32[2048]{0:T(1024)} %param.14) | copy-start | bytes 24580
  0.6 17.1 %copy-start.7 = (bf16[64,256]{1,0:T(8,128)(2,1)S(1)}, bf16[64,256]{1,0:T(8,128)(2,1)}, u32[]{:S(2)}) copy-start(bf16[64,256]{1,0:T(8,128)(2,1)} %wb_ref.3) | copy-start | bytes 98308
  0.7 17.1 %copy-start.5 = (bf16[64,2048]{1,0:T(8,128)(2,1)S(1)}, bf16[64,2048]{1,0:T(8,128)(2,1)}, u32[]{:S(2)}) copy-start(bf16[64,2048]{1,0:T(8,128)(2,1)} %basis_ref.3) | copy-start | bytes 786436
  0.7 17.0 %copy-start.8 = (s32[2048]{0:T(1024)S(1)}, s32[2048]{0:T(1024)}, u32[]{:S(2)}) copy-start(s32[2048]{0:T(1024)} %param.15) | copy-start | bytes 24580
  2.8 7.3 %collective-permute-start = (bf16[1024,256]{1,0:T(8,128)(2,1)}, bf16[1024,256]{1,0:T(8,128)(2,1)S(1)}, u32[]{:S(2)}, u32[]{:S(2)}) collective-permute-start(bf16[1024,256]{1,0:T(8,128)(2,1)} %cot_own_hbm.1), channel_id=1, source_target_pairs={{0,1},{1,0},{2,3},{3,2},{4,5},{5,4},{6,7},{7,6},{8,9},{9,8},{10,11... | collective-permute-start | bytes 1572872 | tf_op jit(solution)/shard_map/ppermute | solution.py:205
  3.2 14.5 %all-to-all-start = ((bf16[8,32,256]{2,1,0:T(8,128)(2,1)}), bf16[8,32,256]{2,1,0:T(8,128)(2,1)S(1)}, u32[]{:S(2)}, u32[]{:S(2)}) async-start(bf16[8,32,256]{2,1,0:T(8,128)(2,1)} %bitcast.6), calls=%async_computation | async-start | bytes 262144 | tf_op jit(solution)/shard_map/all_to_all | solution.py:204
  10.1 1.0 %copy-start = (bf16[1024,256]{1,0:T(8,128)(2,1)S(1)}, bf16[1024,256]{1,0:T(8,128)(2,1)}, u32[]{:S(2)}) copy-start(bf16[1024,256]{1,0:T(8,128)(2,1)} %edges_ref.1) | copy-start | bytes 1572868
  11.2 1.0 %copy-start.1 = (bf16[1024,256]{1,0:T(8,128)(2,1)S(1)}, bf16[1024,256]{1,0:T(8,128)(2,1)}, u32[]{:S(2)}) copy-start(bf16[1024,256]{1,0:T(8,128)(2,1)} %cot_own_hbm.1) | copy-start | bytes 1572868
  12.2 0.7 %copy-start.2 = (s32[2048]{0:T(1024)S(1)}, s32[2048]{0:T(1024)}, u32[]{:S(2)}) copy-start(s32[2048]{0:T(1024)} %param.14) | copy-start | bytes 24580
  17.7 3.1 %copy-start.6 = (bf16[256,512]{1,0:T(8,128)(2,1)S(1)}, bf16[256,512]{1,0:T(8,128)(2,1)}, u32[]{:S(2)}) copy-start(bf16[256,512]{1,0:T(8,128)(2,1)} %w_ref.3) | copy-start | bytes 786436
  20.7 2.4 %collective-permute-start.1 = (bf16[1024,256]{1,0:T(8,128)(2,1)S(1)}, bf16[1024,256]{1,0:T(8,128)(2,1)S(1)}, u32[]{:S(2)}, u32[]{:S(2)}) collective-permute-start(bf16[1024,256]{1,0:T(8,128)(2,1)S(1)} %get-tuple-element.20.own_ref), channel_id=1, source_target_pairs={{0,1},{1,0},{2,3},{3,2},{4,5},{5,4},{6,7},{7,6},{8,9},{9,8},{10,11... | collective-permute-start | bytes 1572872 | tf_op jit(solution)/shard_map/ppermute | solution.py:224
  20.8 2.3 %collective-permute-start.2 = (bf16[256,512]{1,0:T(8,128)(2,1)S(1)}, bf16[256,512]{1,0:T(8,128)(2,1)S(1)}, u32[]{:S(2)}, u32[]{:S(2)}) collective-permute-start(bf16[256,512]{1,0:T(8,128)(2,1)S(1)} %copy-done.6), channel_id=1, source_target_pairs={{0,1},{1,0},{2,3},{3,2},{4,5},{5,4},{6,7},{7,6},{8,9},{9,8},{10,11... | collective-permute-start | bytes 786440 | tf_op jit(solution)/shard_map/ppermute | solution.py:205
  25.0 5.0 %collective-permute-start.3 = (bf16[256,256]{1,0:T(8,128)(2,1)S(1)}, bf16[256,256]{1,0:T(8,128)(2,1)S(1)}, u32[]{:S(2)}, u32[]{:S(2)}) collective-permute-start(bf16[256,256]{1,0:T(8,128)(2,1)S(1)} %get-tuple-element.29), channel_id=1, source_target_pairs={{0,2},{1,5},{2,0},{3,7},{4,6},{5,1},{6,4},{7,3},{8,10},{9,13},{10,... | collective-permute-start | bytes 393224 | tf_op jit(solution)/shard_map/ppermute | solution.py:181
  30.1 6.4 %collective-permute-start.4 = (bf16[320,256]{1,0:T(8,128)(2,1)S(1)}, bf16[320,256]{1,0:T(8,128)(2,1)S(1)}, u32[]{:S(2)}, u32[]{:S(2)}) collective-permute-start(bf16[320,256]{1,0:T(8,128)(2,1)S(1)} %pad_maximum_fusion), channel_id=1, source_target_pairs={{0,4},{1,9},{2,6},{3,11},{4,0},{5,13},{6,2},{7,15},{8,12},{9,1},{1... | collective-permute-start | bytes 491528 | tf_op jit(solution)/shard_map/ppermute | solution.py:181
  36.5 7.7 %collective-permute-start.5 = (bf16[320,256]{1,0:T(8,128)(2,1)S(1)}, bf16[320,256]{1,0:T(8,128)(2,1)S(1)}, u32[]{:S(2)}, u32[]{:S(2)}) collective-permute-start(bf16[320,256]{1,0:T(8,128)(2,1)S(1)} %add_convert_fusion.1), channel_id=1, source_target_pairs={{0,8},{1,3},{2,10},{3,1},{4,12},{5,7},{6,14},{7,5},{8,0},{9,11},{1... | collective-permute-start | bytes 491528 | tf_op jit(solution)/shard_map/ppermute | solution.py:181
  37.6 12.0 %all-to-all-start.1 = ((bf16[8,32,256]{2,1,0:T(8,128)(2,1)}), bf16[8,32,256]{2,1,0:T(8,128)(2,1)S(1)}, u32[]{:S(2)}, u32[]{:S(2)}) async-start(bf16[8,32,256]{2,1,0:T(8,128)(2,1)} %bitcast.8), calls=%async_computation.1 | async-start | bytes 262144 | tf_op jit(solution)/shard_map/all_to_all | solution.py:249
  44.3 5.6 %copy-start.4 = (s32[1,256]{1,0:T(1,128)S(1)}, s32[1,256]{1,0:T(1,128)}, u32[]{:S(2)}) copy-start(s32[1,256]{1,0:T(1,128)} %param.13) | copy-start | bytes 3076
  44.3 5.6 %collective-permute-start.6 = (bf16[320,256]{1,0:T(8,128)(2,1)S(1)}, bf16[320,256]{1,0:T(8,128)(2,1)S(1)}, u32[]{:S(2)}, u32[]{:S(2)}) collective-permute-start(bf16[320,256]{1,0:T(8,128)(2,1)S(1)} %add_convert_fusion.mine_ref), channel_id=1, source_target_pairs={{0,2},{1,5},{2,0},{3,7},{4,6},{5,1},{6,4},{7,3},{8,10},{9,13},{10,... | collective-permute-start | bytes 491528 | tf_op jit(solution)/shard_map/ppermute | solution.py:181
